TPU v7x, 32 devices: a whole 2x2x4 slice. The times are simulated.
32 devices in a mesh: recv: 8 (over z, y), send: 4 (over x, core).
Axes of the slice: x: 2, y: 2, z: 4, core: 2. Of those that a mesh axis runs over, the one named last changes fastest.
Arguments:
- nodes: bfloat16 [4096, 256], P('recv'), may hold values from -24 to 24
- frames: int32 [4096], replicated, may hold values from 0 to 59, never falling along the last dimension, each value on 1 to 256 neighbouring positions
- pairs: int32 [2, 128], P(None, ('recv', 'send')), may hold values from 0 to 31, as said below
- masks: int32 [128, 128], P(('recv', 'send')), may hold values from 0 to 1, as said below
- d_out: bfloat16 [4096, 256], P('recv'), may hold values from -6 to 6
- w_query: bfloat16 [256, 256], replicated, may hold values from -0.375 to 0.375
- w_key: bfloat16 [256, 256], replicated, may hold values from -0.375 to 0.375
- w_value: bfloat16 [256, 256], replicated, may hold values from -0.375 to 0.375
- w_left: bfloat16 [256, 128], replicated, may hold values from -0.375 to 0.375
- w_right: bfloat16 [256, 128], replicated, may hold values from -0.375 to 0.375
- frame_edge: bfloat16 [128], replicated, may hold values from -4 to 4
- w_bias: bfloat16 [8, 128], replicated, may hold values from -0.5 to 0.5
- w_edge_value: bfloat16 [128, 256], replicated, may hold values from -0.5 to 0.5
- w_out: bfloat16 [256, 256], replicated, may hold values from -0.375 to 0.375
Outputs:
- mixed: bfloat16 [4096, 256], P('recv')
- grad_nodes: float32 [4096, 256], P('recv')
- grad_bias: float32 [8, 128], replicated
- grad_edge_value: float32 [128, 256], replicated
Inputs may be any that keep to these rules, and one draw needn't show every extreme that they name: `pairs`: row 0 holds a slot's receiver block, row 1 its sender block; block b belongs to recv index b // 4. The slots of the device at recv index r have receiver blocks r * 4 to r * 4 + 3. The sender blocks of one receiver block are distinct over all its slots and include the block itself, in a slot at send index 0. On each device, the slots whose sender block belongs to another recv index name blocks of distinct recv indices. `masks`: A slot that pairs a block with itself is all ones; other slots may be all zeros. `frames`: frame ids never fall along the residues; every frame holds a residue.
All inputs are finite; a program needn't handle non-finite values.
Results may differ from a plain program's by a relative error of at most 0.039.
Values may be sent and summed in bfloat16 or wider, within the bound.
A program may use at most 128 MiB of HBM per device.

v0:
```python
import jax
import jax.numpy as jnp
from jax import lax
from jax.sharding import PartitionSpec as P

NEG_LARGE = -1e30


def combined_all(value, axis, join):
    pieces = jax.tree.map(lambda part: lax.all_gather(part, axis), value)
    head = jax.tree.map(lambda part: part[0], pieces)
    tail = jax.tree.map(lambda part: part[1:], pieces)
    total, _ = lax.scan(lambda total, piece: (join(total, piece), None), head, tail)
    return total


def highest(grad_rows, weight):
    return jnp.dot(grad_rows, weight.astype(jnp.float32).T, precision=lax.Precision.HIGHEST)


def add_rows(array, start, update):
    current = lax.dynamic_slice_in_dim(array, start, update.shape[0], 0)
    return lax.dynamic_update_slice_in_dim(array, current + update, start, 0)


def combine_stats(first, second):
    first_top, first_total = first
    second_top, second_total = second
    joined = jnp.maximum(first_top, second_top)
    return (
        joined,
        first_total * jnp.exp(first_top - joined) + second_total * jnp.exp(second_top - joined),
    )


def body(
    nodes,
    frames,
    pairs,
    masks,
    d_out,
    w_query,
    w_key,
    w_value,
    w_left,
    w_right,
    frame_edge,
    w_bias,
    w_edge_value,
    w_out,
):
    rows, width = nodes.shape
    block = masks.shape[1]
    nb_local = rows // block
    slot_count = masks.shape[0]
    head_count, edge_width = w_bias.shape
    att_width = w_query.shape[1]
    head_dim = att_width // head_count
    scale = head_dim ** (-0.5)
    my_recv = lax.axis_index("recv")
    n_recv = lax.axis_size("recv")
    base_row = my_recv * rows
    base_block = my_recv * nb_local

    def project(inputs, weight):
        return jnp.dot(inputs, weight, preferred_element_type=jnp.float32).astype(jnp.bfloat16)

    query = project(nodes, w_query)
    left_here = project(nodes, w_left)
    keys_here = project(nodes, w_key)
    values_here = project(nodes, w_value)
    right_here = project(nodes, w_right)
    send_blocks = pairs[1]
    owners = send_blocks // nb_local
    remote = owners != my_recv
    owner_ids = jnp.arange(n_recv, dtype=jnp.int32)
    hits = (owners[None, :] == owner_ids[:, None]) & remote[None, :]
    wanted = jnp.sum(jnp.where(hits, (send_blocks % nb_local)[None, :], 0), axis=1)
    requested = lax.all_to_all(wanted, "recv", split_axis=0, concat_axis=0, tiled=True)
    replies = (
        jnp.take(keys_here.reshape(nb_local, block, att_width), requested, axis=0),
        jnp.take(values_here.reshape(nb_local, block, att_width), requested, axis=0),
        jnp.take(right_here.reshape(nb_local, block, edge_width), requested, axis=0),
    )
    keys_got, values_got, right_got = (
        lax.all_to_all(replies[0], "recv", split_axis=0, concat_axis=0, tiled=True),
        lax.all_to_all(replies[1], "recv", split_axis=0, concat_axis=0, tiled=True),
        lax.all_to_all(replies[2], "recv", split_axis=0, concat_axis=0, tiled=True),
    )
    keys_all = jnp.concatenate([keys_here, keys_got.reshape(n_recv * block, att_width)], axis=0)
    values_all = jnp.concatenate(
        [values_here, values_got.reshape(n_recv * block, att_width)], axis=0
    )
    right_all = jnp.concatenate([right_here, right_got.reshape(n_recv * block, edge_width)], axis=0)

    def table_start(sender):
        owner = sender // nb_local
        return jnp.where(
            owner == my_recv, (sender - base_block) * block, (nb_local + owner) * block
        )

    node_count = keys_all.shape[0]
    frames_here = lax.dynamic_slice_in_dim(frames, base_row, rows)
    edge_gain = frame_edge.astype(jnp.float32)

    def rows_of(array, start):
        return lax.dynamic_slice_in_dim(array, start, block, 0)

    def fetch(slot_at):
        local_block = pairs[0, slot_at] - base_block
        recv_start = local_block * block
        send_start = table_start(pairs[1, slot_at])
        frame_start = pairs[1, slot_at] * block
        query_blk = rows_of(query, recv_start).reshape(block, head_count, head_dim)
        keys_blk = rows_of(keys_all, send_start).reshape(block, head_count, head_dim)
        values_blk = rows_of(values_all, send_start).reshape(block, head_count, head_dim)
        same_frame = (
            rows_of(frames_here, recv_start)[:, None] == rows_of(frames, frame_start)[None, :]
        ).astype(jnp.float32)
        pre_act = (
            rows_of(left_here, recv_start).astype(jnp.float32)[:, None, :]
            + rows_of(right_all, send_start).astype(jnp.float32)[None, :, :]
            + same_frame[:, :, None] * edge_gain[None, None, :]
        )
        edge_feat = jax.nn.silu(pre_act).astype(jnp.bfloat16)
        valid = masks[slot_at] > 0
        logits = (
            jnp.einsum("ihd,jhd->hij", query_blk, keys_blk, preferred_element_type=jnp.float32)
            * scale
        )
        logits = logits + jnp.einsum(
            "ije,he->hij", edge_feat, w_bias, preferred_element_type=jnp.float32
        )
        logits = jnp.where(valid[None, None, :], logits, NEG_LARGE)
        return (
            local_block,
            recv_start,
            send_start,
            query_blk,
            keys_blk,
            values_blk,
            pre_act,
            edge_feat,
            valid,
            logits,
        )

    def skip_empty(slot_at, work, carry):
        return lax.cond(jnp.any(masks[slot_at] > 0), work, lambda state: state, carry)

    def stats_step(slot_at, carry):

        def work(state):
            row_top, row_total = state
            (
                local_block,
                recv_start,
                send_start,
                query_blk,
                keys_blk,
                values_blk,
                pre_act,
                edge_feat,
                valid,
                logits,
            ) = fetch(slot_at)
            slot_top = jnp.max(logits, axis=2)
            slot_total = jnp.sum(
                jnp.where(valid[None, None, :], jnp.exp(logits - slot_top[:, :, None]), 0.0), axis=2
            )
            joined_top, joined_total = combine_stats(
                (row_top[local_block], row_total[local_block]), (slot_top, slot_total)
            )
            return (
                row_top.at[local_block].set(joined_top),
                row_total.at[local_block].set(joined_total),
            )

        return skip_empty(slot_at, work, carry)

    start_stats = (
        jnp.full((nb_local, head_count, block), NEG_LARGE, jnp.float32),
        jnp.zeros((nb_local, head_count, block), jnp.float32),
    )
    local_top, local_total = lax.fori_loop(0, slot_count, stats_step, start_stats)
    row_top, row_total = combined_all((local_top, local_total), "send", combine_stats)

    def probs_of(logits, valid, local_block):
        return jnp.where(
            valid[None, None, :],
            jnp.exp(logits - row_top[local_block][:, :, None]) / row_total[local_block][:, :, None],
            0.0,
        )

    def sum_step(slot_at, carry):

        def work(state):
            out_acc, ctx_acc = state
            (
                local_block,
                recv_start,
                send_start,
                query_blk,
                keys_blk,
                values_blk,
                pre_act,
                edge_feat,
                valid,
                logits,
            ) = fetch(slot_at)
            weights = probs_of(logits, valid, local_block).astype(jnp.bfloat16)
            part_out = jnp.einsum(
                "hij,jhd->ihd", weights, values_blk, preferred_element_type=jnp.float32
            ).reshape(block, att_width)
            part_ctx = jnp.einsum(
                "hij,ije->ihe", weights, edge_feat, preferred_element_type=jnp.float32
            ).reshape(block, head_count * edge_width)
            return (
                add_rows(out_acc, recv_start, part_out),
                add_rows(ctx_acc, recv_start, part_ctx),
            )

        return skip_empty(slot_at, work, carry)

    start_sums = (
        jnp.zeros((rows, att_width), jnp.float32),
        jnp.zeros((rows, head_count * edge_width), jnp.float32),
    )
    local_out, local_ctx = lax.fori_loop(0, slot_count, sum_step, start_sums)
    edge_value = w_edge_value.reshape(edge_width, head_count, head_dim)
    edge_value_f = edge_value.astype(jnp.float32)
    d_att = jnp.dot(d_out, w_out.T, preferred_element_type=jnp.float32).astype(jnp.bfloat16)
    d_att_heads = d_att.reshape(rows, head_count, head_dim)
    d_ctx = jnp.einsum(
        "ihd,ehd->ihe", d_att_heads, edge_value, preferred_element_type=jnp.float32
    ).astype(jnp.bfloat16)
    d_att_f = d_att_heads.astype(jnp.float32)
    d_ctx_f = d_ctx.astype(jnp.float32)
    out_sum, ctx_sum = lax.psum((local_out, local_ctx), "send")
    count = ctx_sum.shape[0]
    attended = (
        out_sum
        + jnp.einsum(
            "ihe,ehd->ihd",
            ctx_sum.reshape(count, head_count, edge_width),
            edge_value_f,
            precision=lax.Precision.HIGHEST,
        ).reshape(count, att_width)
    ).astype(jnp.bfloat16)
    delta = jnp.sum(d_att_f * out_sum.reshape(rows, head_count, head_dim), axis=2) + jnp.sum(
        d_ctx_f * ctx_sum.reshape(rows, head_count, edge_width), axis=2
    )
    share = rows // lax.axis_size("send")
    share_start = lax.axis_index("send") * share
    ctx_rows = lax.dynamic_slice_in_dim(ctx_sum, share_start, share, 0)
    count = ctx_rows.shape[0]
    grad_edge_part = jnp.einsum(
        "ihe,ihd->ehd",
        ctx_rows.reshape(count, head_count, edge_width),
        lax.dynamic_slice_in_dim(d_att_f, share_start, share, 0),
        precision=lax.Precision.HIGHEST,
    ).reshape(edge_width, att_width)
    mixed = (
        nodes.astype(jnp.float32) + jnp.dot(attended, w_out, preferred_element_type=jnp.float32)
    ).astype(jnp.bfloat16)

    def grad_step(slot_at, carry):

        def work(state):
            grad_query, grad_left, grad_keys, grad_values, grad_right, bias_acc = state
            (
                local_block,
                recv_start,
                send_start,
                query_blk,
                keys_blk,
                values_blk,
                pre_act,
                edge_feat,
                valid,
                logits,
            ) = fetch(slot_at)
            probs = probs_of(logits, valid, local_block)
            weights = probs.astype(jnp.bfloat16)
            datt_blk = rows_of(d_att_heads, recv_start)
            dctx_blk = rows_of(d_ctx, recv_start)
            delta_blk = rows_of(delta, recv_start)
            d_prob = jnp.einsum(
                "ihd,jhd->hij", datt_blk, values_blk, preferred_element_type=jnp.float32
            ) + jnp.einsum("ihe,ije->hij", dctx_blk, edge_feat, preferred_element_type=jnp.float32)
            d_logit = jnp.where(
                valid[None, None, :], probs * (d_prob - delta_blk.T[:, :, None]), 0.0
            ).astype(jnp.bfloat16)
            part_query = (
                jnp.einsum("hij,jhd->ihd", d_logit, keys_blk, preferred_element_type=jnp.float32)
                * scale
            ).reshape(block, att_width)
            part_keys = (
                jnp.einsum("hij,ihd->jhd", d_logit, query_blk, preferred_element_type=jnp.float32)
                * scale
            ).reshape(block, att_width)
            part_values = jnp.einsum(
                "hij,ihd->jhd", weights, datt_blk, preferred_element_type=jnp.float32
            ).reshape(block, att_width)
            bias_acc = bias_acc + jnp.einsum(
                "hij,ije->he", d_logit, edge_feat, preferred_element_type=jnp.float32
            )
            d_edge = jnp.einsum(
                "hij,he->ije", d_logit, w_bias, preferred_element_type=jnp.float32
            ) + jnp.einsum("hij,ihe->ije", weights, dctx_blk, preferred_element_type=jnp.float32)
            sigmoid_v = jax.nn.sigmoid(pre_act)
            d_pre = (d_edge * sigmoid_v * (1.0 + pre_act * (1.0 - sigmoid_v))).astype(jnp.bfloat16)
            grad_query = add_rows(grad_query, recv_start, part_query)
            grad_left = add_rows(grad_left, recv_start, jnp.sum(d_pre, axis=1, dtype=jnp.float32))
            grad_keys = add_rows(grad_keys, send_start, part_keys)
            grad_values = add_rows(grad_values, send_start, part_values)
            grad_right = add_rows(grad_right, send_start, jnp.sum(d_pre, axis=0, dtype=jnp.float32))
            return (grad_query, grad_left, grad_keys, grad_values, grad_right, bias_acc)

        return skip_empty(slot_at, work, carry)

    start_grads = (
        jnp.zeros((rows, att_width), jnp.float32),
        jnp.zeros((rows, edge_width), jnp.float32),
        jnp.zeros((node_count, att_width), jnp.float32),
        jnp.zeros((node_count, att_width), jnp.float32),
        jnp.zeros((node_count, edge_width), jnp.float32),
        jnp.zeros((head_count, edge_width), jnp.float32),
    )
    grad_query, grad_left, grad_keys, grad_values, grad_right, bias_part = lax.fori_loop(
        0, slot_count, grad_step, start_grads
    )
    receiver_part = highest(grad_query, w_query) + highest(grad_left, w_left)
    returning = (
        grad_keys[rows:].reshape(n_recv, block, att_width),
        grad_values[rows:].reshape(n_recv, block, att_width),
        grad_right[rows:].reshape(n_recv, block, edge_width),
    )
    keys_back, values_back, right_back = (
        lax.all_to_all(
            returning[0].astype(jnp.bfloat16), "recv", split_axis=0, concat_axis=0, tiled=True
        ).astype(jnp.float32),
        lax.all_to_all(
            returning[1].astype(jnp.bfloat16), "recv", split_axis=0, concat_axis=0, tiled=True
        ).astype(jnp.float32),
        lax.all_to_all(
            returning[2].astype(jnp.bfloat16), "recv", split_axis=0, concat_axis=0, tiled=True
        ).astype(jnp.float32),
    )
    placing = (requested[:, None] == jnp.arange(nb_local, dtype=jnp.int32)[None, :]).astype(
        jnp.float32
    )

    def settle(own_rows, returned):
        landed = jnp.einsum("rb,rkc->bkc", placing, returned, precision=lax.Precision.HIGHEST)
        return own_rows + landed.reshape(rows, returned.shape[2])

    node_part = (
        receiver_part
        + highest(settle(grad_keys[:rows], keys_back), w_key)
        + highest(settle(grad_values[:rows], values_back), w_value)
        + highest(settle(grad_right[:rows], right_back), w_right)
    )
    grad_nodes = d_out.astype(jnp.float32) + lax.psum(node_part, "send")
    grad_bias, grad_edge_value = lax.psum((bias_part, grad_edge_part), ("recv", "send"))
    return (mixed, grad_nodes, grad_bias, grad_edge_value)


def solution(mesh):
    in_specs = (
        P("recv", None),
        P(),
        P(None, ("recv", "send")),
        P(("recv", "send"), None),
        P("recv", None),
        P(),
        P(),
        P(),
        P(),
        P(),
        P(),
        P(),
        P(),
        P(),
    )
    out_specs = (P("recv", None), P("recv", None), P(), P())
    return jax.shard_map(body, mesh=mesh, in_specs=in_specs, out_specs=out_specs, check_vma=False)
```

profile of v0, /device:TPU:0, one launch (start us, length us, event | category | flops | bytes accessed | tf_op | source)
XLA Modules:
  0.0 650.4 jit_solution(17078417913002371949)
XLA Ops:
  8.8 7.3 %all-to-all-start = ((s32[8,1,1]{2,1,0:T(1,128)}), s32[8,1,1]{2,1,0:T(1,128)S(1)}, u32[]{:S(2)}, u32[]{:S(2)}) async-start(s32[8,1,1]{2,1,0:T(1,128)} %copy.141), calls=%async_computation | async-start | bytes 8192 | tf_op jit(solution)/shard_map/all_to_all | solution.py:79
  19.7 2.7 all-to-all-done
  24.1 3.4 all-to-all-start.3
  29.7 6.2 all-to-all-done.3
  35.9 17.2 %all_to_all.45 = bf16[8,128,256]{2,1,0:T(8,128)(2,1)S(1)} all-to-all(bf16[8,128,256]{2,1,0:T(8,128)(2,1)S(1)} %get-tuple-element.1678), channel_id=1, replica_groups=mesh['recv'=8,'send'=4] {'recv'}, dimensions={0} | all-to-all | bytes 1048576 | tf_op jit(solution)/shard_map/all_to_all | solution.py:86
  53.1 3.6 all-to-all-start.1
  60.1 10.7 %all-to-all-done.1 = bf16[8,128,256]{2,1,0:T(8,128)(2,1)S(1)} async-done(((bf16[8,128,256]{2,1,0:T(8,128)(2,1)}), bf16[8,128,256]{2,1,0:T(8,128)(2,1)S(1)}, u32[]{:S(2)}, u32[]{:S(2)}) %all-to-all-start.1) | async-done | bytes 524320 | tf_op jit(solution)/shard_map/all_to_all | solution.py:87
  73.1 50.1 %while.67 = (s32[]{:T(128)}, f32[4,8,128]{2,1,0:T(8,128)S(1)}, f32[4,8,128]{2,1,0:T(8,128)S(1)}, s32[4,128]{1,0:T(4,128)S(1)}, s32[2,4]{1,0:T(2,128)S(1)}, /*ind...) while((s32[]{:T(128)}, f32[4,8,128]{2,1,0:T(8,128)S(1)}, ...), condition=%wide.region_8.10_spmd, body=%wide.region_1.9_spmd.sunk | while | flops 59709880 | bytes 4042427 | solution.py:185
  74.4 11.2 %conditional.6 = ((f32[4,8,128]{2,1,0:T(8,128)S(1)}, f32[4,8,128]{2,1,0:T(8,128)S(1)})) conditional(s32[]{:T(128)} %convert_element_type.216, (f32[4,8,128]{2,1,0:T(8,128)S(1)}, f32[4,8,128]{2,1,0:T(8,128)S(1)}) %tuple.161, (s32[]{:T(128)}, s32[2,4]{1,0:T(2,128)S(1)}, s32[]{:T(128)}, f32[4,8,128]{2,1,0:T(8,128)S(1)}, s32[4,128]{1,0:T(4,128)S(1)}, ...), branch_computations={%region_3.4_spmd, %region_4.8_spmd} | conditional | flops 59709624 | bytes 4041612 | solution.py:149
  86.9 11.2 %conditional.6 = ((f32[4,8,128]{2,1,0:T(8,128)S(1)}, f32[4,8,128]{2,1,0:T(8,128)S(1)})) conditional(s32[]{:T(128)} %convert_element_type.216, (f32[4,8,128]{2,1,0:T(8,128)S(1)}, f32[4,8,128]{2,1,0:T(8,128)S(1)}) %tuple.161, (s32[]{:T(128)}, s32[2,4]{1,0:T(2,128)S(1)}, s32[]{:T(128)}, f32[4,8,128]{2,1,0:T(8,128)S(1)}, s32[4,128]{1,0:T(4,128)S(1)}, ...), branch_computations={%region_3.4_spmd, %region_4.8_spmd} | conditional | flops 59709624 | bytes 4041612 | solution.py:149
  99.4 11.2 %conditional.6 = ((f32[4,8,128]{2,1,0:T(8,128)S(1)}, f32[4,8,128]{2,1,0:T(8,128)S(1)})) conditional(s32[]{:T(128)} %convert_element_type.216, (f32[4,8,128]{2,1,0:T(8,128)S(1)}, f32[4,8,128]{2,1,0:T(8,128)S(1)}) %tuple.161, (s32[]{:T(128)}, s32[2,4]{1,0:T(2,128)S(1)}, s32[]{:T(128)}, f32[4,8,128]{2,1,0:T(8,128)S(1)}, s32[4,128]{1,0:T(4,128)S(1)}, ...), branch_computations={%region_3.4_spmd, %region_4.8_spmd} | conditional | flops 59709624 | bytes 4041612 | solution.py:149
  111.9 11.2 %conditional.6 = ((f32[4,8,128]{2,1,0:T(8,128)S(1)}, f32[4,8,128]{2,1,0:T(8,128)S(1)})) conditional(s32[]{:T(128)} %convert_element_type.216, (f32[4,8,128]{2,1,0:T(8,128)S(1)}, f32[4,8,128]{2,1,0:T(8,128)S(1)}) %tuple.161, (s32[]{:T(128)}, s32[2,4]{1,0:T(2,128)S(1)}, s32[]{:T(128)}, f32[4,8,128]{2,1,0:T(8,128)S(1)}, s32[4,128]{1,0:T(4,128)S(1)}, ...), branch_computations={%region_3.4_spmd, %region_4.8_spmd} | conditional | flops 59709624 | bytes 4041612 | solution.py:149
  123.7 5.2 all-gather.1
  129.0 5.4 all-gather
  135.4 79.3 %while.69 = (s32[]{:T(128)}, f32[512,256]{0,1:T(8,128)S(1)}, f32[512,1024]{1,0:T(8,128)S(1)}, s32[4,128]{1,0:T(4,128)}, s32[2,4]{1,0:T(2,128)}, /*index=5*/s32[]...) while((s32[]{:T(128)}, f32[512,256]{0,1:T(8,128)S(1)}, ...), condition=%wide.region_15.17_spmd, body=%wide.region_11.16_spmd.sunk | while | flops 118587808 | bytes 5737113 | solution.py:229
  137.4 17.8 %conditional.7 = ((f32[512,256]{0,1:T(8,128)S(1)}, f32[512,1024]{1,0:T(8,128)S(1)})) conditional(s32[]{:T(128)} %convert_element_type.217, (f32[512,256]{0,1:T(8,128)S(1)}, f32[512,1024]{1,0:T(8,128)S(1)}) %tuple.166, (s32[]{:T(128)}, s32[2,4]{1,0:T(2,128)}, s32[]{:T(128)}, f32[512,256]{0,1:T(8,128)S(1)}, s32[]{:T(128)}, ...), branch_computations={%region_13.14_spmd, %region_14.15_spmd} | conditional | flops 118587552 | bytes 5736250 | solution.py:149
  148.5 3.2 fusion.16
  152.4 2.6 fusion.15
  157.2 17.8 %conditional.7 = ((f32[512,256]{0,1:T(8,128)S(1)}, f32[512,1024]{1,0:T(8,128)S(1)})) conditional(s32[]{:T(128)} %convert_element_type.217, (f32[512,256]{0,1:T(8,128)S(1)}, f32[512,1024]{1,0:T(8,128)S(1)}) %tuple.166, (s32[]{:T(128)}, s32[2,4]{1,0:T(2,128)}, s32[]{:T(128)}, f32[512,256]{0,1:T(8,128)S(1)}, s32[]{:T(128)}, ...), branch_computations={%region_13.14_spmd, %region_14.15_spmd} | conditional | flops 118587552 | bytes 5736250 | solution.py:149
  168.3 3.2 fusion.16
  177.1 17.8 %conditional.7 = ((f32[512,256]{0,1:T(8,128)S(1)}, f32[512,1024]{1,0:T(8,128)S(1)})) conditional(s32[]{:T(128)} %convert_element_type.217, (f32[512,256]{0,1:T(8,128)S(1)}, f32[512,1024]{1,0:T(8,128)S(1)}) %tuple.166, (s32[]{:T(128)}, s32[2,4]{1,0:T(2,128)}, s32[]{:T(128)}, f32[512,256]{0,1:T(8,128)S(1)}, s32[]{:T(128)}, ...), branch_computations={%region_13.14_spmd, %region_14.15_spmd} | conditional | flops 118587552 | bytes 5736250 | solution.py:149
  188.1 3.2 fusion.16
  192.1 2.6 fusion.15
  196.9 17.8 %conditional.7 = ((f32[512,256]{0,1:T(8,128)S(1)}, f32[512,1024]{1,0:T(8,128)S(1)})) conditional(s32[]{:T(128)} %convert_element_type.217, (f32[512,256]{0,1:T(8,128)S(1)}, f32[512,1024]{1,0:T(8,128)S(1)}) %tuple.166, (s32[]{:T(128)}, s32[2,4]{1,0:T(2,128)}, s32[]{:T(128)}, f32[512,256]{0,1:T(8,128)S(1)}, s32[]{:T(128)}, ...), branch_computations={%region_13.14_spmd, %region_14.15_spmd} | conditional | flops 118587552 | bytes 5736250 | solution.py:149
  207.9 3.2 fusion.16
  217.6 58.3 %all-reduce.9.cloned.1.call-done = (f32[512,256]{0,1:T(8,128)}, f32[512,1024]{0,1:T(8,128)}) async-done(((f32[512,256]{0,1:T(8,128)}, f32[512,1024]{0,1:T(8,128)}), (f32[512,256]{0,1:T(8,128)}, f32[512,1024]{0,1:T(8,128)})) %all-reduce.9.cloned.1.call-update) | async-done | bytes 2621456 | tf_op jit(solution)/shard_map/psum | solution.py:239
  284.6 133.7 %while.70 = (s32[]{:T(128)}, f32[512,256]{0,1:T(8,128)S(1)}, f32[512,128]{1,0:T(8,128)S(1)}, f32[1536,256]{0,1:T(8,128)}, f32[1536,256]{0,1:T(8,128)}, /*index=5...) while((s32[]{:T(128)}, f32[512,256]{0,1:T(8,128)S(1)}, ...), condition=%wide.region_26.28_spmd, body=%wide.region_20.27_spmd.sunk | while | flops 295404960 | bytes 26599216 | solution.py:330
  286.3 32.0 %conditional.8 = ((f32[512,256]{0,1:T(8,128)S(1)}, f32[512,128]{1,0:T(8,128)S(1)}, f32[1536,256]{0,1:T(8,128)}, f32[1536,256]{0,1:T(8,128)}, f32[1536,128]{1,0:T(8,128)}, /*index=5*/f32[8,128]{1,0:T(8,128)})) conditional(s32[]{:T(128)} %convert_element_type.218, (f32[512,256]{0,1:T(8,128)S(1)}, f32[512,128]{1,0:T(8,128)S(1)}, ...), branch_computations={%region_22.23_spmd, %region_23.26_spmd} | conditional | flops 295404704 | bytes 26598210 | solution.py:149
  302.3 3.9 fusion.43
  310.2 6.5 %convert_reduce_fusion = (f32[128,128]{1,0:T(8,128)S(1)}, f32[128,128]{1,0:T(8,128)S(1)}) fusion(f32[128]{0:T(128)S(1)} %get-tuple-element.1154, f32[128,128]{1,0:T(8,128)S(1)} %compare_convert_fusion.2, f32[128,128]{1,0:T(8,128)S(1)} %dynamic-slice_convert_fusion.4, f32[128,128]{1,0:T(8,128)S(1)} %dynamic-slice_convert_fusion.5, ...), kind=kOutput, calls=%fused_computation.70 | convolution fusion | flops 67076096 | bytes 9241092 | tf_op jit(solution)/shard_map/while/body/eval_jaxpr/cond/branch_1_fun/hij,ihe->ije/dot_general | solution.py:310
  319.7 31.9 %conditional.8 = ((f32[512,256]{0,1:T(8,128)S(1)}, f32[512,128]{1,0:T(8,128)S(1)}, f32[1536,256]{0,1:T(8,128)}, f32[1536,256]{0,1:T(8,128)}, f32[1536,128]{1,0:T(8,128)}, /*index=5*/f32[8,128]{1,0:T(8,128)})) conditional(s32[]{:T(128)} %convert_element_type.218, (f32[512,256]{0,1:T(8,128)S(1)}, f32[512,128]{1,0:T(8,128)S(1)}, ...), branch_computations={%region_22.23_spmd, %region_23.26_spmd} | conditional | flops 295404704 | bytes 26598210 | solution.py:149
  335.7 3.9 fusion.43
  343.6 6.5 %convert_reduce_fusion = (f32[128,128]{1,0:T(8,128)S(1)}, f32[128,128]{1,0:T(8,128)S(1)}) fusion(f32[128]{0:T(128)S(1)} %get-tuple-element.1154, f32[128,128]{1,0:T(8,128)S(1)} %compare_convert_fusion.2, f32[128,128]{1,0:T(8,128)S(1)} %dynamic-slice_convert_fusion.4, f32[128,128]{1,0:T(8,128)S(1)} %dynamic-slice_convert_fusion.5, ...), kind=kOutput, calls=%fused_computation.70 | convolution fusion | flops 67076096 | bytes 9241092 | tf_op jit(solution)/shard_map/while/body/eval_jaxpr/cond/branch_1_fun/hij,ihe->ije/dot_general | solution.py:310
  353.0 32.0 %conditional.8 = ((f32[512,256]{0,1:T(8,128)S(1)}, f32[512,128]{1,0:T(8,128)S(1)}, f32[1536,256]{0,1:T(8,128)}, f32[1536,256]{0,1:T(8,128)}, f32[1536,128]{1,0:T(8,128)}, /*index=5*/f32[8,128]{1,0:T(8,128)})) conditional(s32[]{:T(128)} %convert_element_type.218, (f32[512,256]{0,1:T(8,128)S(1)}, f32[512,128]{1,0:T(8,128)S(1)}, ...), branch_computations={%region_22.23_spmd, %region_23.26_spmd} | conditional | flops 295404704 | bytes 26598210 | solution.py:149
  369.1 3.9 fusion.43
  376.9 6.5 %convert_reduce_fusion = (f32[128,128]{1,0:T(8,128)S(1)}, f32[128,128]{1,0:T(8,128)S(1)}) fusion(f32[128]{0:T(128)S(1)} %get-tuple-element.1154, f32[128,128]{1,0:T(8,128)S(1)} %compare_convert_fusion.2, f32[128,128]{1,0:T(8,128)S(1)} %dynamic-slice_convert_fusion.4, f32[128,128]{1,0:T(8,128)S(1)} %dynamic-slice_convert_fusion.5, ...), kind=kOutput, calls=%fused_computation.70 | convolution fusion | flops 67076096 | bytes 9241092 | tf_op jit(solution)/shard_map/while/body/eval_jaxpr/cond/branch_1_fun/hij,ihe->ije/dot_general | solution.py:310
  386.4 32.0 %conditional.8 = ((f32[512,256]{0,1:T(8,128)S(1)}, f32[512,128]{1,0:T(8,128)S(1)}, f32[1536,256]{0,1:T(8,128)}, f32[1536,256]{0,1:T(8,128)}, f32[1536,128]{1,0:T(8,128)}, /*index=5*/f32[8,128]{1,0:T(8,128)})) conditional(s32[]{:T(128)} %convert_element_type.218, (f32[512,256]{0,1:T(8,128)S(1)}, f32[512,128]{1,0:T(8,128)S(1)}, ...), branch_computations={%region_22.23_spmd, %region_23.26_spmd} | conditional | flops 295404704 | bytes 26598210 | solution.py:149
  402.4 3.9 fusion.43
  410.3 6.5 %convert_reduce_fusion = (f32[128,128]{1,0:T(8,128)S(1)}, f32[128,128]{1,0:T(8,128)S(1)}) fusion(f32[128]{0:T(128)S(1)} %get-tuple-element.1154, f32[128,128]{1,0:T(8,128)S(1)} %compare_convert_fusion.2, f32[128,128]{1,0:T(8,128)S(1)} %dynamic-slice_convert_fusion.4, f32[128,128]{1,0:T(8,128)S(1)} %dynamic-slice_convert_fusion.5, ...), kind=kOutput, calls=%fused_computation.70 | convolution fusion | flops 67076096 | bytes 9241092 | tf_op jit(solution)/shard_map/while/body/eval_jaxpr/cond/branch_1_fun/hij,ihe->ije/dot_general | solution.py:310
  420.3 5.5 all-to-all-start.6
  425.8 3.0 copy.153
  430.9 3.1 copy.157
  436.0 6.0 all-to-all-start.4
  448.8 6.2 all-to-all-done.4
  455.0 3.7 all-to-all-start.5
  464.6 7.8 %all-to-all-done.5 = bf16[8,128,256]{2,1,0:T(8,128)(2,1)S(1)} async-done(((bf16[8,128,256]{2,1,0:T(8,128)(2,1)}), bf16[8,128,256]{2,1,0:T(8,128)(2,1)S(1)}, u32[]{:S(2)}, u32[]{:S(2)}) %all-to-all-start.5) | async-done | bytes 524320 | tf_op jit(solution)/shard_map/all_to_all | solution.py:343
  479.2 38.6 %psum.38 = f32[8,128]{1,0:T(8,128)} all-reduce(f32[8,128]{1,0:T(8,128)} %get-tuple-element.1226), channel_id=1, replica_groups=mesh['recv'=8,'send'=4] {'recv','send'}, use_global_device_ids=true, to_apply=%region_28.30 | all-reduce | flops 1024 | bytes 8192 | tf_op jit(solution)/shard_map/psum | solution.py:365
  521.7 120.6 %all-reduce.7.cloned.1.call-done = f32[128,256]{1,0:T(8,128)} async-done(((f32[128,256]{1,0:T(8,128)}), f32[128,256]{1,0:T(8,128)}) %all-reduce.7.cloned.1.call-update) | async-done | bytes 131088 | tf_op jit(solution)/shard_map/psum | solution.py:365
  (366 shorter events, 198.3 us)
Async XLA Ops:
  7.2 268.8 %copy-start = (bf16[256,256]{1,0:T(8,128)(2,1)S(1)}, bf16[256,256]{1,0:T(8,128)(2,1)}, u32[]{:S(2)}) copy-start(bf16[256,256]{1,0:T(8,128)(2,1)} %param.47) | copy-start | bytes 393220
  7.2 51.3 %copy-start.2 = (bf16[512,256]{1,0:T(8,128)(2,1)S(1)}, bf16[512,256]{1,0:T(8,128)(2,1)}, u32[]{:S(2)}) copy-start(bf16[512,256]{1,0:T(8,128)(2,1)} %param.34) | copy-start | bytes 786436
  7.2 51.3 %copy-start.23 = (bf16[128]{0:T(256)(128)(2,1)S(1)}, bf16[128]{0:T(256)(128)(2,1)}, u32[]{:S(2)}) copy-start(bf16[128]{0:T(256)(128)(2,1)} %param.44) | copy-start | bytes 772
  7.2 51.3 %copy-start.12 = (bf16[256,256]{1,0:T(8,128)(2,1)S(1)}, bf16[256,256]{1,0:T(8,128)(2,1)}, u32[]{:S(2)}) copy-start(bf16[256,256]{1,0:T(8,128)(2,1)} %param.39) | copy-start | bytes 393220
  7.2 52.4 %copy-start.13 = (bf16[256,128]{1,0:T(8,128)(2,1)S(1)}, bf16[256,128]{1,0:T(8,128)(2,1)}, u32[]{:S(2)}) copy-start(bf16[256,128]{1,0:T(8,128)(2,1)} %param.42) | copy-start | bytes 196612
  8.8 13.7 %all-to-all-start = ((s32[8,1,1]{2,1,0:T(1,128)}), s32[8,1,1]{2,1,0:T(1,128)S(1)}, u32[]{:S(2)}, u32[]{:S(2)}) async-start(s32[8,1,1]{2,1,0:T(1,128)} %copy.141), calls=%async_computation | async-start | bytes 8192 | tf_op jit(solution)/shard_map/all_to_all | solution.py:79
  19.7 53.4 %copy-start.14 = (s32[2,4]{1,0:T(2,128)S(1)}, s32[2,4]{1,0:T(2,128)}, u32[]{:S(2)}) copy-start(s32[2,4]{1,0:T(2,128)} %param.36) | copy-start | bytes 100
  19.7 53.4 %copy-start.16 = (bf16[8,128]{1,0:T(8,128)(2,1)S(1)}, bf16[8,128]{1,0:T(8,128)(2,1)}, u32[]{:S(2)}) copy-start(bf16[8,128]{1,0:T(8,128)(2,1)} %param.45) | copy-start | bytes 6148
  19.7 53.4 %copy-start.21 = (s32[4,128]{1,0:T(4,128)S(1)}, s32[4,128]{1,0:T(4,128)}, u32[]{:S(2)}) copy-start(s32[4,128]{1,0:T(4,128)} %param.37) | copy-start | bytes 6148
  22.7 36.2 %copy-start.18 = (s32[8]{0:T(128)}, s32[8]{0:T(128)S(1)}, u32[]{:S(2)}) copy-start(s32[8]{0:T(128)S(1)} %reduce.11) | copy-start | bytes 100
  24.1 11.8 %all-to-all-start.3 = ((bf16[8,128,128]{2,1,0:T(8,128)(2,1)}), bf16[8,128,128]{2,1,0:T(8,128)(2,1)S(1)}, u32[]{:S(2)}, u32[]{:S(2)}) async-start(bf16[8,128,128]{2,1,0:T(8,128)(2,1)} %broadcast_select_fusion.2), calls=%async_computation.3 | async-start | bytes 524288 | tf_op jit(solution)/shard_map/all_to_all | solution.py:88
  53.1 17.7 %all-to-all-start.1 = ((bf16[8,128,256]{2,1,0:T(8,128)(2,1)}), bf16[8,128,256]{2,1,0:T(8,128)(2,1)S(1)}, u32[]{:S(2)}, u32[]{:S(2)}) async-start(bf16[8,128,256]{2,1,0:T(8,128)(2,1)} %get-tuple-element.1679), calls=%async_computation.1 | async-start | bytes 1048576 | tf_op jit(solution)/shard_map/all_to_all | solution.py:87
  56.7 219.2 %all-reduce.9.cloned.1.call-start = ((), (), s32[]{:S(2)}) async-start(), calls=%async_computation.9 | async-start | bytes 5242880 | tf_op jit(solution)/shard_map/psum | solution.py:239
  123.2 0.6 copy-start.25
  123.2 11.4 %copy-start.5 = (bf16[1536,256]{0,1:T(8,128)(2,1)}, bf16[1536,256]{0,1:T(8,128)(2,1)S(1)}, u32[]{:S(2)}) copy-start(bf16[1536,256]{0,1:T(8,128)(2,1)S(1)} %get-tuple-element.2337) | copy-start | bytes 2359300
  123.2 11.4 %copy-start.20 = (s32[512]{0:T(512)}, s32[512]{0:T(512)S(1)}, u32[]{:S(2)}) copy-start(s32[512]{0:T(512)S(1)} %get-tuple-element.2371) | copy-start | bytes 6148
  134.5 0.6 copy-start.9
  148.5 3.2 copy-start.24
  148.5 3.9 copy-start.26
  168.3 3.2 copy-start.24
  168.3 4.0 copy-start.26
  188.1 3.2 copy-start.24
  188.1 3.9 copy-start.26
  207.9 3.2 copy-start.24
  207.9 4.0 copy-start.26
  214.7 1.9 copy-start.4
  214.7 65.5 %copy-start.8 = (bf16[1536,128]{1,0:T(8,128)(2,1)}, bf16[1536,128]{1,0:T(8,128)(2,1)S(1)}, u32[]{:S(2)}) copy-start(bf16[1536,128]{1,0:T(8,128)(2,1)S(1)} %get-tuple-element.2353) | copy-start | bytes 1179652
  216.6 68.1 %copy-start.15 = (s32[2,4]{1,0:T(2,128)S(1)}, s32[2,4]{1,0:T(2,128)}, u32[]{:S(2)}) copy-start(s32[2,4]{1,0:T(2,128)} %get-tuple-element.2364) | copy-start | bytes 100
  216.6 68.1 %copy-start.17 = (bf16[8,128]{1,0:T(8,128)(2,1)S(1)}, bf16[8,128]{1,0:T(8,128)(2,1)}, u32[]{:S(2)}) copy-start(bf16[8,128]{1,0:T(8,128)(2,1)} %get-tuple-element.2369) | copy-start | bytes 6148
  216.6 68.1 %copy-start.22 = (s32[4,128]{1,0:T(4,128)S(1)}, s32[4,128]{1,0:T(4,128)}, u32[]{:S(2)}) copy-start(s32[4,128]{1,0:T(4,128)} %get-tuple-element.2376) | copy-start | bytes 6148
  216.6 68.1 %copy-start.27 = (f32[128]{0:T(128)S(1)}, f32[128]{0:T(128)}, u32[]{:S(2)}) copy-start(f32[128]{0:T(128)} %get-tuple-element.2378) | copy-start | bytes 1540
  217.6 61.8 %copy-start.11 = (bf16[128,256]{0,1:T(8,128)(2,1)}, bf16[128,256]{0,1:T(8,128)(2,1)S(1)}, u32[]{:S(2)}) copy-start(bf16[128,256]{0,1:T(8,128)(2,1)S(1)} %copy.149) | copy-start | bytes 196612
  418.3 23.7 %copy-start.1 = (f32[512,1024]{0,1:T(8,128)S(1)}, f32[512,1024]{0,1:T(8,128)}, u32[]{:S(2)}) copy-start(f32[512,1024]{0,1:T(8,128)} %get-tuple-element.1646) | copy-start | bytes 6291460
  420.3 15.7 %all-to-all-start.6 = ((bf16[8,128,128]{2,1,0:T(8,128)(2,1)}), bf16[8,128,128]{2,1,0:T(8,128)(2,1)S(1)}, u32[]{:S(2)}, u32[]{:S(2)}) async-start(bf16[8,128,128]{2,1,0:T(8,128)(2,1)} %bitcast.209), calls=%async_computation.6 | async-start | bytes 524288 | tf_op jit(solution)/shard_map/all_to_all | solution.py:346
  425.8 32.9 %copy-start.19 = (s32[8]{0:T(128)S(1)}, s32[8]{0:T(128)}, u32[]{:S(2)}) copy-start(s32[8]{0:T(128)} %copy-done.18) | copy-start | bytes 100
  436.0 9.2 %copy-start.10 = (bf16[8,128,128]{2,1,0:T(8,128)(2,1)}, bf16[8,128,128]{2,1,0:T(8,128)(2,1)S(1)}, u32[]{:S(2)}) copy-start(bf16[8,128,128]{2,1,0:T(8,128)(2,1)S(1)} %all-to-all-done.6) | copy-start | bytes 786436
  436.0 19.0 %all-to-all-start.4 = ((bf16[8,128,256]{2,1,0:T(8,128)(2,1)}), bf16[8,128,256]{2,1,0:T(8,128)(2,1)}, u32[]{:S(2)}, u32[]{:S(2)}) async-start(bf16[8,128,256]{2,1,0:T(8,128)(2,1)} %bitcast.203), calls=%async_computation.4 | async-start | bytes 1048576 | tf_op jit(solution)/shard_map/all_to_all | solution.py:340
  445.2 29.2 %copy-start.6 = (f32[512,256]{1,0:T(8,128)S(1)}, f32[512,256]{1,0:T(8,128)}, u32[]{:S(2)}) copy-start(f32[512,256]{1,0:T(8,128)} %fusion.92) | copy-start | bytes 1572868
  446.9 31.0 %copy-start.7 = (f32[128,1024]{0,1:T(8,128)S(1)}, f32[128,1024]{0,1:T(8,128)}, u32[]{:S(2)}) copy-start(f32[128,1024]{0,1:T(8,128)} %constant_dynamic-slice_fusion.20) | copy-start | bytes 1572868
  446.9 70.9 %copy-start.3 = (bf16[512,256]{1,0:T(8,128)(2,1)S(1)}, bf16[512,256]{1,0:T(8,128)(2,1)}, u32[]{:S(2)}) copy-start(bf16[512,256]{1,0:T(8,128)(2,1)} %param.34) | copy-start | bytes 786436
  455.0 17.5 %all-to-all-start.5 = ((bf16[8,128,256]{2,1,0:T(8,128)(2,1)}), bf16[8,128,256]{2,1,0:T(8,128)(2,1)S(1)}, u32[]{:S(2)}, u32[]{:S(2)}) async-start(bf16[8,128,256]{2,1,0:T(8,128)(2,1)} %bitcast.200), calls=%async_computation.5 | async-start | bytes 1048576 | tf_op jit(solution)/shard_map/all_to_all | solution.py:343
  458.6 61.1 %all-reduce.5.cloned.1.call-start = ((), (), s32[]{:S(2)}) async-start(), calls=%async_computation.7 | async-start | bytes 1048576 | tf_op jit(solution)/shard_map/psum | solution.py:364
  477.8 164.5 %all-reduce.7.cloned.1.call-start = ((), (), s32[]{:S(2)}) async-start(), calls=%async_computation.8 | async-start | bytes 262144 | tf_op jit(solution)/shard_map/psum | solution.py:365
Sparse Core Ops, SparseCore 0:
  216.7 59.1 all-reduce.8
  477.9 31.6 all-reduce.4
  519.9 122.3 all-reduce.6
where the time goes:
time: 656 us; the launch traced here: 650 us
  waiting for transfers between devices  213 us (32%)
  matrix products  135 us (21%)
  local copies, waits for them, and re-layouts  76.3 us (12%)
  blocking collectives  66.5 us (10%)
  loops' own time  63.5 us (10%)
  other arithmetic  52.3 us (8%)
  starting transfers between devices  29.6 us (5%)
  between operations  14.3 us (2%)
    psum x1, waiting for transfers between devices, body(): lax.psum((bias_part, grad_edge_part), ('recv', 'send'))  121 us
    psum x1, waiting for transfers between devices, body(): out_sum, ctx_sum = lax.psum((local_out, local_ctx), 'send')  58.3 us
    another operation x12, loops' own time, skip_empty(): lax.cond(jnp.any(masks[slot_at] > 0), work, lambda state: state, carry)  55.1 us
    psum x1, blocking collectives, body(): lax.psum((bias_part, grad_edge_part), ('recv', 'send'))  38.6 us
    dot_general x12, matrix products, fetch(): jnp.einsum('ije,he->hij', edge_feat, w_bias, preferred_element_type=jnp.f...  32.9 us
    dynamic_slice x48, local copies, waits for them, and re-layouts, rows_of(): return lax.dynamic_slice_in_dim(array, start, block, 0)  28.8 us
    dot_general x4, matrix products, work(): jnp.einsum('hij,ihe->ije', weights, dctx_blk, preferred_element_type=jnp....  26.2 us
    all_to_all x1, blocking collectives, body(): lax.all_to_all(replies[0], 'recv', split_axis=0, concat_axis=0, tiled=True)  17.2 us
  transfers between devices with their start and end apart: 9, of which 7 were waited for; matrix products, arithmetic and copies ran while one was open for 6% of the time, Pallas kernels for 0%

commit v1 on v0

v1 whole, which is shorter than its diff:
```python
import functools

import jax
import jax.numpy as jnp
from jax import lax
from jax.experimental import pallas as pl
from jax.experimental.pallas import tpu as pltpu
from jax.sharding import PartitionSpec as P

NEG_LARGE = -1e30
CHUNK = 16
F32 = jnp.float32
BF16 = jnp.bfloat16


def dot(first, second, first_dim=1, second_dim=0):
    return lax.dot_general(
        first, second, (((first_dim,), (second_dim,)), ((), ())), preferred_element_type=F32
    )


def to_column(row):
    count = row.shape[1]
    eye = lax.broadcasted_iota(jnp.int32, (count, count), 0) == lax.broadcasted_iota(
        jnp.int32, (count, count), 1
    )
    return jnp.sum(jnp.where(eye, row, 0.0), axis=1, keepdims=True)


def to_row(column):
    count = column.shape[0]
    eye = lax.broadcasted_iota(jnp.int32, (count, count), 0) == lax.broadcasted_iota(
        jnp.int32, (count, count), 1
    )
    return jnp.sum(jnp.where(eye, column, 0.0), axis=0, keepdims=True)


def head_mask(heads, width):
    return lax.broadcasted_iota(jnp.int32, (heads, width), 1) // (
        width // heads
    ) == lax.broadcasted_iota(jnp.int32, (heads, width), 0)


def spread(rows, heads):
    count, width = rows.shape
    mask = head_mask(heads, width)
    wide = jnp.where(mask[None], rows.astype(F32)[:, None, :], 0.0)
    return wide.reshape(count * heads, width).astype(BF16)


def gather_heads(wide, heads):
    count, width = wide.shape
    mask = head_mask(heads, width)
    return jnp.sum(jnp.where(mask[None], wide.reshape(count // heads, heads, width), 0.0), axis=1)


def forward_kernel(
    scale,
    local_ref,
    table_ref,
    recv_ref,
    send_ref,
    frames_ref,
    frame_row_ref,
    mask_ref,
    nodes_ref,
    dout_ref,
    sender_ref,
    wq_ref,
    wk_ref,
    wv_ref,
    wl_ref,
    wr_ref,
    fe_ref,
    wb_ref,
    wev_ref,
    wo_ref,
    logit_ref,
    dprob_ref,
    slope_ref,
    sums_ref,
    wide_ref,
    att_ref,
    stats_ref,
    left_s,
    edge_s,
    probs_s,
):
    slot = pl.program_id(0)
    heads, edge_width = wb_ref.shape
    block = nodes_ref.shape[0]
    nodes = nodes_ref[...]
    sender = sender_ref[0]
    query = dot(nodes, wq_ref[...]).astype(BF16)
    left_s[...] = dot(nodes, wl_ref[...]).astype(BF16).astype(F32) * 0.5
    datt = dot(dout_ref[...], wo_ref[...], 1, 1).astype(BF16)
    keys = dot(sender, wk_ref[...]).astype(BF16)
    values = dot(sender, wv_ref[...]).astype(BF16)
    right = dot(sender, wr_ref[...]).astype(BF16).astype(F32) * 0.5
    right_same = right + fe_ref[...].astype(F32) * 0.5
    frame_col = jnp.broadcast_to(
        to_column(frame_row_ref[0].astype(F32)), (block, edge_width)
    )
    datt_wide = spread(datt, heads)
    logit_ref[0] = (dot(spread(query, heads), keys, 1, 1) * scale).reshape(block, heads, block)
    dprob_ref[0] = dot(datt_wide, values, 1, 1).reshape(block, heads, block)
    dctx = dot(datt_wide, wev_ref[...], 1, 1).reshape(block, heads, edge_width)
    bias = jnp.broadcast_to(wb_ref[...].astype(F32)[None], dctx.shape)
    wide_ref[0] = jnp.concatenate([bias, dctx], axis=1).astype(BF16)
    recv_start = recv_ref[slot] * block

    def edge_step(group, carry):
        start = group * CHUNK
        left_rows = left_s[pl.ds(start, CHUNK), :]
        for step in range(CHUNK):
            at = start + step
            frame = frames_ref[recv_start + at].astype(F32)
            half = left_rows[step : step + 1] + jnp.where(frame_col == frame, right_same, right)
            turn = jnp.tanh(half)
            gain = half * turn
            edge = (half + gain).astype(BF16)
            slope_ref[0, at] = ((1.0 + turn) * (1.0 + half - gain)).astype(BF16)
            edge_s[at] = edge
            both = dot(wide_ref[0, at], edge, 1, 1)
            logit_ref[0, at] = logit_ref[0, at] + both[:heads]
            dprob_ref[0, at] = dprob_ref[0, at] + both[heads:]
        return carry

    lax.fori_loop(0, block // CHUNK, edge_step, 0)
    valid = mask_ref[0] > 0

    def soft_step(group, carry):
        start = group * CHUNK
        rows = pl.ds(start * heads, CHUNK * heads)
        logits = logit_ref[0, pl.ds(start, CHUNK)].reshape(CHUNK * heads, block)
        dprob = dprob_ref[0, pl.ds(start, CHUNK)].reshape(CHUNK * heads, block)
        logits = jnp.where(valid, logits, NEG_LARGE)
        top = jnp.max(logits, axis=1, keepdims=True)
        probs = jnp.where(valid, jnp.exp(logits - top), 0.0)
        weighted = probs * dprob
        stats_ref[0, 0, pl.ds(group, 1), :] = to_row(top)
        stats_ref[0, 1, pl.ds(group, 1), :] = to_row(jnp.sum(probs, axis=1, keepdims=True))
        stats_ref[0, 2, pl.ds(group, 1), :] = to_row(jnp.sum(weighted, axis=1, keepdims=True))
        probs_s[rows, :] = probs.astype(BF16)
        pair = jnp.concatenate(
            [probs.reshape(CHUNK, heads, block), weighted.reshape(CHUNK, heads, block)], axis=1
        ).astype(BF16)
        for step in range(CHUNK):
            at = start + step
            sums_ref[0, at] = dot(pair[step], edge_s[at]).astype(BF16)
        return carry

    lax.fori_loop(0, block // CHUNK, soft_step, 0)
    stats_ref[0, 3] = jnp.full(stats_ref.shape[2:], local_ref[slot].astype(F32), F32)
    ctx = sums_ref[0].astype(F32)[:, :heads].reshape(block * heads, edge_width).astype(BF16)
    att_ref[0] = gather_heads(dot(probs_s[...], values) + dot(ctx, wev_ref[...]), heads)


def backward_kernel(
    scale,
    local_ref,
    table_ref,
    mask_ref,
    nodes_ref,
    dout_ref,
    sender_ref,
    wq_ref,
    wk_ref,
    wv_ref,
    wl_ref,
    wr_ref,
    wo_ref,
    logit_ref,
    dprob_ref,
    slope_ref,
    sums_ref,
    wide_ref,
    att_in_ref,
    stats_ref,
    joined_ref,
    recv_grad_ref,
    send_grad_ref,
    att_ref,
    grad_ev_ref,
    grad_bias_ref,
    probs_s,
    dlogit_s,
    ctx_s,
    left_s,
    right_s,
):
    slot = pl.program_id(0)
    heads = logit_ref.shape[2]
    block = nodes_ref.shape[0]
    edge_width = wide_ref.shape[3]
    width = wq_ref.shape[1]
    mask = head_mask(heads, width)
    valid = mask_ref[0] > 0

    @pl.when(slot == 0)
    def _():
        grad_ev_ref[...] = jnp.zeros_like(grad_ev_ref)
        grad_bias_ref[...] = jnp.zeros_like(grad_bias_ref)

    right_s[...] = jnp.zeros_like(right_s)

    def step_group(group, carry):
        start = group * CHUNK
        rows = pl.ds(start * heads, CHUNK * heads)
        lse = joined_ref[0, 0, pl.ds(group, 1), :]
        lse_col = to_column(lse)
        delta_col = to_column(joined_ref[0, 1, pl.ds(group, 1), :])
        factor_col = to_column(jnp.exp(stats_ref[0, 0, pl.ds(group, 1), :] - lse))
        logits = logit_ref[0, pl.ds(start, CHUNK)].reshape(CHUNK * heads, block)
        dprob = dprob_ref[0, pl.ds(start, CHUNK)].reshape(CHUNK * heads, block)
        probs = jnp.where(valid, jnp.exp(logits - lse_col), 0.0)
        dlogit = probs * (dprob - delta_col)
        probs_s[rows, :] = probs.astype(BF16)
        dlogit_s[rows, :] = dlogit.astype(BF16)
        sums = sums_ref[0, pl.ds(start, CHUNK)].astype(F32)
        ctx = sums[:, :heads].reshape(CHUNK * heads, edge_width) * factor_col
        ctx_s[rows, :] = ctx.astype(BF16)
        moved = sums[:, heads:].reshape(CHUNK * heads, edge_width) * factor_col - ctx * delta_col
        grad_bias_ref[...] += jnp.sum(moved.reshape(CHUNK, heads, edge_width), axis=0)
        factor = jnp.sum(
            jnp.where(mask[None], factor_col.reshape(CHUNK, heads, 1), 0.0), axis=1
        )
        att_ref[0, pl.ds(start, CHUNK), :] = att_in_ref[0, pl.ds(start, CHUNK), :] * factor
        pair = jnp.concatenate(
            [dlogit.reshape(CHUNK, heads, block), probs.reshape(CHUNK, heads, block)], axis=1
        ).astype(BF16)
        right_sum = right_s[...]
        lefts = []
        for step in range(CHUNK):
            at = start + step
            d_edge = dot(pair[step], wide_ref[0, at], 0, 0)
            d_pre = d_edge * slope_ref[0, at].astype(F32)
            right_sum = right_sum + d_pre
            lefts.append(jnp.sum(d_pre, axis=0, keepdims=True))
        right_s[...] = right_sum
        left_s[pl.ds(start, CHUNK), :] = jnp.concatenate(lefts, axis=0)
        return carry

    lax.fori_loop(0, block // CHUNK, step_group, 0)
    nodes = nodes_ref[...]
    sender = sender_ref[0]
    query_wide = spread(dot(nodes, wq_ref[...]).astype(BF16), heads)
    datt_wide = spread(dot(dout_ref[...], wo_ref[...], 1, 1).astype(BF16), heads)
    keys = dot(sender, wk_ref[...]).astype(BF16)
    dlogit = dlogit_s[...]
    grad_query = gather_heads(dot(dlogit, keys), heads) * scale
    grad_keys = dot(dlogit, query_wide, 0, 0) * scale
    grad_values = dot(probs_s[...], datt_wide, 0, 0)
    recv_grad_ref[0] = dot(grad_query.astype(BF16), wq_ref[...], 1, 1) + 0.5 * dot(
        left_s[...].astype(BF16), wl_ref[...], 1, 1
    )
    send_grad_ref[0] = (
        dot(grad_keys.astype(BF16), wk_ref[...], 1, 1)
        + dot(grad_values.astype(BF16), wv_ref[...], 1, 1)
        + 0.5 * dot(right_s[...].astype(BF16), wr_ref[...], 1, 1)
    )
    grad_ev_ref[...] += dot(ctx_s[...], datt_wide, 0, 0)


def whole_spec(array):
    zeros = (0,) * array.ndim
    return pl.BlockSpec(array.shape, lambda slot, *_: zeros)


def slot_spec(shape):
    rest = (0,) * (len(shape) - 1)
    return pl.BlockSpec((1,) + tuple(shape[1:]), lambda slot, *_: (slot,) + rest)


def body(
    nodes,
    frames,
    pairs,
    masks,
    d_out,
    w_query,
    w_key,
    w_value,
    w_left,
    w_right,
    frame_edge,
    w_bias,
    w_edge_value,
    w_out,
):
    rows, width = nodes.shape
    slots, block = masks.shape
    nb_local = rows // block
    heads, edge_width = w_bias.shape
    att_width = w_query.shape[1]
    scale = (att_width // heads) ** (-0.5)
    my_recv = lax.axis_index("recv")
    n_recv = lax.axis_size("recv")
    base_block = my_recv * nb_local

    send_blocks = pairs[1]
    local_blocks = pairs[0] - base_block
    owners = send_blocks // nb_local
    remote = owners != my_recv
    owner_ids = jnp.arange(n_recv, dtype=jnp.int32)
    hits = (owners[None, :] == owner_ids[:, None]) & remote[None, :]
    wanted = jnp.sum(jnp.where(hits, (send_blocks % nb_local)[None, :], 0), axis=1)
    requested = lax.all_to_all(wanted, "recv", split_axis=0, concat_axis=0, tiled=True)
    node_blocks = nodes.reshape(nb_local, block, width)
    got = lax.all_to_all(
        jnp.take(node_blocks, requested, axis=0), "recv", split_axis=0, concat_axis=0, tiled=True
    )
    table = jnp.concatenate([node_blocks, got], axis=0)
    table_at = jnp.where(remote, nb_local + owners, send_blocks - base_block)

    frame_rows = frames.reshape(-1, 1, block)
    mask_rows = masks.reshape(slots, 1, block)
    edge_row = frame_edge.reshape(1, edge_width)
    recv_spec = pl.BlockSpec((block, width), lambda slot, local, *_: (local[slot], 0))
    sender_spec = pl.BlockSpec((1, block, width), lambda slot, local, at, *_: (at[slot], 0, 0))
    logit_shape = (slots, block, heads, block)
    sums_shape = (slots, block, 2 * heads, edge_width)
    slope_shape = (slots, block, block, edge_width)
    att_shape = (slots, block, att_width)
    stats_shape = (slots, 4, block * heads // 128, 128)
    weights = (w_query, w_key, w_value, w_left, w_right, edge_row, w_bias, w_edge_value, w_out)
    forward = pl.pallas_call(
        functools.partial(forward_kernel, scale),
        grid_spec=pltpu.PrefetchScalarGridSpec(
            num_scalar_prefetch=5,
            grid=(slots,),
            in_specs=[
                pl.BlockSpec((1, 1, block), lambda slot, local, at, recv, send, *_: (send[slot], 0, 0)),
                slot_spec(mask_rows.shape),
                recv_spec,
                recv_spec,
                sender_spec,
            ]
            + [whole_spec(weight) for weight in weights],
            out_specs=[
                slot_spec(shape)
                for shape in (
                    logit_shape, logit_shape, slope_shape, sums_shape, sums_shape, att_shape, stats_shape,
                )
            ],
            scratch_shapes=[
                pltpu.VMEM((block, edge_width), F32),
                pltpu.VMEM((block, block, edge_width), BF16),
                pltpu.VMEM((block * heads, block), BF16),
            ],
        ),
        out_shape=[
            jax.ShapeDtypeStruct(logit_shape, F32),
            jax.ShapeDtypeStruct(logit_shape, F32),
            jax.ShapeDtypeStruct(slope_shape, BF16),
            jax.ShapeDtypeStruct(sums_shape, BF16),
            jax.ShapeDtypeStruct(sums_shape, BF16),
            jax.ShapeDtypeStruct(att_shape, F32),
            jax.ShapeDtypeStruct(stats_shape, F32),
        ],
        compiler_params=pltpu.CompilerParams(vmem_limit_bytes=50 * 2**20),
        name="forward",
    )
    logits, dprobs, slopes, sums, wides, att_parts, stats = forward(
        local_blocks, table_at, pairs[0], send_blocks, frames,
        frame_rows, mask_rows, nodes, d_out, table, *weights,
    )

    all_stats = lax.all_gather(stats, "send").reshape((-1,) + stats.shape[1:])
    lands = all_stats[:, 3, 0, 0].astype(jnp.int32)
    here = (lands[None, :] == local_blocks[:, None])[:, :, None, None]
    tops = all_stats[None, :, 0]
    top = jnp.max(jnp.where(here, tops, NEG_LARGE), axis=1)
    shares = jnp.where(here, jnp.exp(tops - top[:, None]), 0.0)
    total = jnp.sum(shares * all_stats[None, :, 1], axis=1)
    delta = jnp.sum(shares * all_stats[None, :, 2], axis=1) / total
    joined = jnp.stack([top + jnp.log(total), delta], axis=1)

    weights = (w_query, w_key, w_value, w_left, w_right, w_out)
    grad_shape = (slots, block, width)
    backward = pl.pallas_call(
        functools.partial(backward_kernel, scale),
        grid_spec=pltpu.PrefetchScalarGridSpec(
            num_scalar_prefetch=2,
            grid=(slots,),
            in_specs=[slot_spec(mask_rows.shape), recv_spec, recv_spec, sender_spec]
            + [whole_spec(weight) for weight in weights]
            + [
                slot_spec(shape)
                for shape in (
                    logit_shape, logit_shape, slope_shape, sums_shape, sums_shape, att_shape, stats_shape,
                    joined.shape,
                )
            ],
            out_specs=[
                slot_spec(grad_shape),
                slot_spec(grad_shape),
                slot_spec(att_shape),
                whole_spec(w_edge_value),
                whole_spec(w_bias),
            ],
            scratch_shapes=[
                pltpu.VMEM((block * heads, block), BF16),
                pltpu.VMEM((block * heads, block), BF16),
                pltpu.VMEM((block * heads, edge_width), BF16),
                pltpu.VMEM((block, edge_width), F32),
                pltpu.VMEM((block, edge_width), F32),
            ],
        ),
        out_shape=[
            jax.ShapeDtypeStruct(grad_shape, F32),
            jax.ShapeDtypeStruct(grad_shape, F32),
            jax.ShapeDtypeStruct(att_shape, F32),
            jax.ShapeDtypeStruct(w_edge_value.shape, F32),
            jax.ShapeDtypeStruct(w_bias.shape, F32),
        ],
        compiler_params=pltpu.CompilerParams(vmem_limit_bytes=50 * 2**20),
        name="backward",
    )
    recv_grads, send_grads, att, grad_ev, grad_bias = backward(
        local_blocks, table_at, mask_rows, nodes, d_out, table, *weights,
        logits, dprobs, slopes, sums, wides, att_parts, stats, joined,
    )

    block_ids = jnp.arange(nb_local, dtype=jnp.int32)
    to_recv = (local_blocks[None, :] == block_ids[:, None])[:, :, None, None]
    own = (~remote & ((send_blocks - base_block)[None, :] == block_ids[:, None]))[:, :, None, None]
    away = hits[:, :, None, None]
    leaving = jnp.sum(jnp.where(away, send_grads[None], 0.0), axis=1).astype(BF16)
    back = lax.all_to_all(leaving, "recv", split_axis=0, concat_axis=0, tiled=True)
    landing = (requested[None, :] == block_ids[:, None])[:, :, None, None]
    node_part = (
        jnp.sum(jnp.where(to_recv, recv_grads[None], 0.0), axis=1)
        + jnp.sum(jnp.where(own, send_grads[None], 0.0), axis=1)
        + jnp.sum(jnp.where(landing, back[None].astype(F32), 0.0), axis=1)
    ).reshape(rows, width)
    att_part = jnp.sum(jnp.where(to_recv, att[None], 0.0), axis=1).reshape(rows, att_width)
    attended, node_grad = lax.psum((att_part, node_part), "send")
    mixed = (
        nodes.astype(F32) + jnp.dot(attended.astype(BF16), w_out, preferred_element_type=F32)
    ).astype(BF16)
    grad_nodes = d_out.astype(F32) + node_grad
    grad_bias, grad_ev = lax.psum((grad_bias, grad_ev), ("recv", "send"))
    return (mixed, grad_nodes, grad_bias, grad_ev)


def solution(mesh):
    in_specs = (
        P("recv", None),
        P(),
        P(None, ("recv", "send")),
        P(("recv", "send"), None),
        P("recv", None),
        P(),
        P(),
        P(),
        P(),
        P(),
        P(),
        P(),
        P(),
        P(),
    )
    out_specs = (P("recv", None), P("recv", None), P(), P())
    return jax.shard_map(body, mesh=mesh, in_specs=in_specs, out_specs=out_specs, check_vma=False)
```

time: 656 us -> 320 us (0.49)
  matrix products: 135 us -> 0.94 us
  local copies, waits for them, and re-layouts: 76.3 us -> 3.39 us
  waiting for transfers between devices: 213 us -> 148 us
  loops' own time: 63.5 us -> 0 us
  Pallas kernels: 0 us -> 60.1 us
  other arithmetic: 52.3 us -> 9.1 us
  starting transfers between devices: 29.6 us -> 7.24 us
  blocking collectives: 66.5 us -> 76.9 us
    dot_general x82 -> x1, matrix products: 135 us -> 0.94 us  [body(): jnp.dot(attended.astype(BF16), w_out, preferred_element_type=F32)]
    another operation x16 -> x0, loops' own time: 63.5 us -> none  [the longest x12 55.1 us: skip_empty(): lax.cond(jnp.any(masks[slot_at] > 0), work, lambda state: state, carry)]
    pallas_call x0 -> x2, Pallas kernels: none -> 60.1 us  [the longest x1 35.1 us: body(): forward(local_blocks, table_at, pairs[0], send_blocks, frames, frame_rows...]
    psum x3 -> x2, waiting for transfers between devices: 179 us -> 121 us  [the longest x1 121 us: body(): grad_bias, grad_ev = lax.psum((grad_bias, grad_ev), ('recv', 'send'))]
    dynamic_slice x62 -> x0, local copies, waits for them, and re-layouts: 40.9 us -> none  [the longest x48 28.8 us: rows_of(): return lax.dynamic_slice_in_dim(array, start, block, 0)]
    all_to_all x6 -> x2, starting transfers between devices: 29.5 us -> 7.16 us  [the longest x1 3.66 us: body(): lax.all_to_all(leaving, 'recv', split_axis=0, concat_axis=0, tiled=True)]
    psum x1 -> x2, blocking collectives: 38.6 us -> 57.6 us  [the longest x1 38.3 us: body(): grad_bias, grad_ev = lax.psum((grad_bias, grad_ev), ('recv', 'send'))]
    dynamic_update_slice x20 -> x0, other arithmetic: 13.9 us -> none  [add_rows(): return lax.dynamic_update_slice_in_dim(array, current + update, start, 0)]
  transfers between devices with their start and end apart: 9 -> 4, of which waited for: 7 -> 3; matrix products, arithmetic and copies ran while one was open for 6% -> 1% of each run, Pallas kernels for 0% -> 0%
where the time goes in v1:
time: 320 us
  waiting for transfers between devices  148 us (46%)
  blocking collectives  76.9 us (24%)
  Pallas kernels  60.1 us (19%)
  between operations  14.4 us (4%)
  other arithmetic  9.1 us (3%)
  starting transfers between devices  7.24 us (2%)
  local copies, waits for them, and re-layouts  3.39 us (1%)
    psum x1, waiting for transfers between devices, body(): grad_bias, grad_ev = lax.psum((grad_bias, grad_ev), ('recv', 'send'))  121 us
    psum x1, blocking collectives, body(): grad_bias, grad_ev = lax.psum((grad_bias, grad_ev), ('recv', 'send'))  38.3 us
    pallas_call x1, Pallas kernels, body(): forward(local_blocks, table_at, pairs[0], send_blocks, frames, frame_rows...  35.1 us
    pallas_call x1, Pallas kernels, body(): backward(local_blocks, table_at, mask_rows, nodes, d_out, table, *weights...  25.1 us
    psum x1, blocking collectives, body(): attended, node_grad = lax.psum((att_part, node_part), 'send')  19.3 us
    all_to_all x1, blocking collectives, body(): lax.all_to_all(wanted, 'recv', split_axis=0, concat_axis=0, tiled=True)  13.5 us
    all_to_all x1, waiting for transfers between devices, body(): lax.all_to_all(leaving, 'recv', split_axis=0, concat_axis=0, tiled=True)  13.4 us
    all_to_all x1, waiting for transfers between devices, body(): lax.all_to_all(jnp.take(node_blocks, requested, axis=0), 'recv', split_ax...  13.1 us
  transfers between devices with their start and end apart: 4, of which 3 were waited for; matrix products, arithmetic and copies ran while one was open for 1% of the time, Pallas kernels for 0%

profile of v1, /device:TPU:0, one launch (start us, length us, event | category | flops | bytes accessed | tf_op | source)
XLA Modules:
  0.0 319.8 jit_solution(4274080266685641739)
XLA Ops:
  7.2 0.0 copy-start
  7.2 0.7 not_bitcast_fusion
  8.0 0.1 select_reduce_fusion.6
  8.0 0.1 copy.24
  8.1 13.5 %all_to_all.25 = s32[8,1,1]{2,1,0:T(1,128)S(1)} all-to-all(s32[8,1,1]{2,1,0:T(1,128)S(1)} %copy.24), channel_id=1, replica_groups=mesh['recv'=8,'send'=4] {'recv'}, dimensions={0} | all-to-all | bytes 64 | tf_op jit(solution)/shard_map/all_to_all | solution.py:308
  21.7 0.2 reduce
  21.9 1.5 gather_fusion
  23.5 0.0 copy-start.2
  23.5 0.0 copy-start.3
  23.5 0.0 copy-start.4
  23.5 0.0 copy-start.5
  23.5 0.0 copy-start.6
  23.5 0.0 copy-start.7
  23.5 0.0 copy-start.8
  23.6 0.0 copy-start.9
  23.6 0.0 copy-start.10
  23.6 0.0 copy-start.11
  23.6 0.0 copy-start.13
  23.6 0.9 broadcast_select_fusion
  24.5 3.5 %all-to-all-start.1 = ((bf16[8,128,256]{2,1,0:T(8,128)(2,1)}), bf16[8,128,256]{2,1,0:T(8,128)(2,1)S(1)}, u32[]{:S(2)}, u32[]{:S(2)}) async-start(bf16[8,128,256]{2,1,0:T(8,128)(2,1)} %broadcast_select_fusion), calls=%async_computation.1 | async-start | bytes 1048576 | tf_op jit(solution)/shard_map/all_to_all | solution.py:310
  28.0 0.1 copy.25
  28.2 13.1 %all-to-all-done.1 = bf16[8,128,256]{2,1,0:T(8,128)(2,1)S(1)} async-done(((bf16[8,128,256]{2,1,0:T(8,128)(2,1)}), bf16[8,128,256]{2,1,0:T(8,128)(2,1)S(1)}, u32[]{:S(2)}, u32[]{:S(2)}) %all-to-all-start.1) | async-done | bytes 524320 | tf_op jit(solution)/shard_map/all_to_all | solution.py:310
  41.3 0.1 pad_maximum_fusion.sender_ref
  41.5 35.1 %forward.1 = (f32[4,128,8,128]{3,2,1,0:T(8,128)}, f32[4,128,8,128]{3,2,1,0:T(8,128)}, bf16[4,128,128,128]{3,2,1,0:T(8,128)(2,1)}, bf16[4,128,16,128]{3,2,1,0:T(8...) custom-call(s32[4]{0:T(128)S(1)} %get-tuple-element.47.local_ref, ...), custom_call_target="tpu_custom_call" | custom-call | tf_op jit(solution)/shard_map/forward/pallas_call | solution.py:364
  76.6 5.8 %all-gather = f32[16,4,8,128]{3,2,1,0:T(8,128)S(1)} all-gather(f32[4,4,8,128]{3,2,1,0:T(8,128)S(1)} %get-tuple-element.22.stats_ref), channel_id=2, replica_groups=mesh['recv'=8,'send'=4] {'send'}, dimensions={0}, use_global_device_ids=true | all-gather | bytes 327680 | tf_op jit(solution)/shard_map/all_gather | solution.py:369
  82.3 0.4 fusion.2
  82.7 0.1 broadcast_compare_fusion
  82.8 0.1 select_reduce_fusion.5
  83.0 0.1 multiply_reduce_fusion.1
  83.1 25.1 %backward.1 = (f32[4,128,256]{2,1,0:T(8,128)S(1)}, f32[4,128,256]{2,1,0:T(8,128)S(1)}, f32[4,128,256]{2,1,0:T(8,128)S(1)}, f32[128,256]{1,0:T(8,128)}, f32[8,128]{1,0:T(8,128)S(1)}) custom-call(s32[4]{0:T(128)S(1)} %get-tuple-element.47.local_ref, s32[4]{0:T(128)S(1)} %get-tuple-element.46.table_ref, s32[4,1,128]{2,1,0:T(1,128)S(1)} %bitcast.45, ...), custom_call_target="tpu_custom_call" | custom-call | tf_op jit(solution)/shard_map/backward/pallas_call | solution.py:420
  108.2 1.4 select_reduce_fusion.1
  109.6 3.7 %all-to-all-start.2 = ((bf16[8,128,256]{2,1,0:T(8,128)(2,1)}), bf16[8,128,256]{2,1,0:T(8,128)(2,1)S(1)}, u32[]{:S(2)}, u32[]{:S(2)}) async-start(bf16[8,128,256]{2,1,0:T(8,128)(2,1)} %select_reduce_fusion.1), calls=%async_computation.2 | async-start | bytes 1048576 | tf_op jit(solution)/shard_map/all_to_all | solution.py:430
  113.2 0.0 all-reduce.4.cloned.1.call-start
  113.3 1.5 select_reduce_fusion.3
  114.8 13.4 %all-to-all-done.2 = bf16[8,128,256]{2,1,0:T(8,128)(2,1)S(1)} async-done(((bf16[8,128,256]{2,1,0:T(8,128)(2,1)}), bf16[8,128,256]{2,1,0:T(8,128)(2,1)S(1)}, u32[]{:S(2)}, u32[]{:S(2)}) %all-to-all-start.2) | async-done | bytes 524320 | tf_op jit(solution)/shard_map/all_to_all | solution.py:430
  128.3 0.1 convert_element_type.36
  128.4 0.5 select_reduce_fusion
  128.9 0.9 add_add_fusion
  129.8 0.0 all-reduce.4.cloned.1.call-update
  129.8 0.0 all-reduce.6.cloned.1.call-start
  129.8 19.3 %all-reduce.7 = bf16[512,256]{1,0:T(8,128)(2,1)S(1)} all-reduce(f32[512,256]{1,0:T(8,128)S(1)} %bitcast.47), channel_id=1, replica_groups=mesh['recv'=8,'send'=4] {'send'}, use_global_device_ids=true, to_apply=%region_5.6 | all-reduce | flops 131072 | bytes 786432 | tf_op jit(solution)/shard_map/psum | solution.py:438
  149.2 38.3 %psum.30 = f32[8,128]{1,0:T(8,128)} all-reduce(f32[8,128]{1,0:T(8,128)S(1)} %get-tuple-element.26), channel_id=1, replica_groups=mesh['recv'=8,'send'=4] {'recv','send'}, use_global_device_ids=true, to_apply=%region_11.12 | all-reduce | flops 1024 | bytes 8192 | tf_op jit(solution)/shard_map/psum | solution.py:443
  187.5 0.9 fusion
  188.4 0.0 all-reduce.6.cloned.1.call-update
  188.4 0.0 all-reduce.4.cloned.1.call-done
  188.4 1.9 convert_add_fusion
  190.3 121.0 %all-reduce.6.cloned.1.call-done = f32[128,256]{1,0:T(8,128)} async-done(((f32[128,256]{1,0:T(8,128)}), f32[128,256]{1,0:T(8,128)}) %all-reduce.6.cloned.1.call-update) | async-done | bytes 131088 | tf_op jit(solution)/shard_map/psum | solution.py:443
  311.3 1.6 copy.30
  (35 shorter events, 0.2 us)
Async XLA Ops:
  7.2 21.0 %copy-start.16 = (s32[2,4]{1,0:T(2,128)S(1)}, s32[2,4]{1,0:T(2,128)}, u32[]{:S(2)}) copy-start(s32[2,4]{1,0:T(2,128)} %param.16) | copy-start | bytes 100
  7.2 34.1 %copy-start = (bf16[512,256]{1,0:T(8,128)(2,1)S(1)}, bf16[512,256]{1,0:T(8,128)(2,1)}, u32[]{:S(2)}) copy-start(bf16[512,256]{1,0:T(8,128)(2,1)} %nodes_ref.3) | copy-start | bytes 786436
  23.5 17.9 %copy-start.2 = (bf16[512,256]{1,0:T(8,128)(2,1)S(1)}, bf16[512,256]{1,0:T(8,128)(2,1)}, u32[]{:S(2)}) copy-start(bf16[512,256]{1,0:T(8,128)(2,1)} %dout_ref.3) | copy-start | bytes 786436
  23.5 17.9 %copy-start.3 = (bf16[256,256]{1,0:T(8,128)(2,1)S(1)}, bf16[256,256]{1,0:T(8,128)(2,1)}, u32[]{:S(2)}) copy-start(bf16[256,256]{1,0:T(8,128)(2,1)} %wo_ref.3) | copy-start | bytes 393220
  23.5 17.9 %copy-start.4 = (bf16[256,256]{1,0:T(8,128)(2,1)S(1)}, bf16[256,256]{1,0:T(8,128)(2,1)}, u32[]{:S(2)}) copy-start(bf16[256,256]{1,0:T(8,128)(2,1)} %wq_ref.3) | copy-start | bytes 393220
  23.5 17.9 %copy-start.5 = (bf16[256,256]{1,0:T(8,128)(2,1)S(1)}, bf16[256,256]{1,0:T(8,128)(2,1)}, u32[]{:S(2)}) copy-start(bf16[256,256]{1,0:T(8,128)(2,1)} %wk_ref.3) | copy-start | bytes 393220
  23.5 17.9 %copy-start.6 = (bf16[256,256]{1,0:T(8,128)(2,1)S(1)}, bf16[256,256]{1,0:T(8,128)(2,1)}, u32[]{:S(2)}) copy-start(bf16[256,256]{1,0:T(8,128)(2,1)} %wv_ref.3) | copy-start | bytes 393220
  23.5 17.9 %copy-start.7 = (bf16[256,128]{1,0:T(8,128)(2,1)S(1)}, bf16[256,128]{1,0:T(8,128)(2,1)}, u32[]{:S(2)}) copy-start(bf16[256,128]{1,0:T(8,128)(2,1)} %wl_ref.3) | copy-start | bytes 196612
  23.5 17.9 %copy-start.8 = (bf16[256,128]{1,0:T(8,128)(2,1)S(1)}, bf16[256,128]{1,0:T(8,128)(2,1)}, u32[]{:S(2)}) copy-start(bf16[256,128]{1,0:T(8,128)(2,1)} %wr_ref.3) | copy-start | bytes 196612
  23.6 17.9 %copy-start.9 = (s32[4096]{0:T(1024)S(1)}, s32[4096]{0:T(1024)}, u32[]{:S(2)}) copy-start(s32[4096]{0:T(1024)} %frames_ref.1) | copy-start | bytes 49156
  23.6 17.9 %copy-start.10 = (bf16[128,256]{1,0:T(8,128)(2,1)S(1)}, bf16[128,256]{1,0:T(8,128)(2,1)}, u32[]{:S(2)}) copy-start(bf16[128,256]{1,0:T(8,128)(2,1)} %wev_ref.1) | copy-start | bytes 196612
  23.6 17.9 %copy-start.11 = (s32[4,128]{1,0:T(4,128)S(1)}, s32[4,128]{1,0:T(4,128)}, u32[]{:S(2)}) copy-start(s32[4,128]{1,0:T(4,128)} %param.17) | copy-start | bytes 6148
  23.6 17.9 %copy-start.12 = (bf16[8,128]{1,0:T(8,128)(2,1)S(1)}, bf16[8,128]{1,0:T(8,128)(2,1)}, u32[]{:S(2)}) copy-start(bf16[8,128]{1,0:T(8,128)(2,1)} %wb_ref.1) | copy-start | bytes 6148
  23.6 17.9 %copy-start.13 = (bf16[128]{0:T(256)(128)(2,1)S(1)}, bf16[128]{0:T(256)(128)(2,1)}, u32[]{:S(2)}) copy-start(bf16[128]{0:T(256)(128)(2,1)} %param.24) | copy-start | bytes 772
  24.5 16.8 %all-to-all-start.1 = ((bf16[8,128,256]{2,1,0:T(8,128)(2,1)}), bf16[8,128,256]{2,1,0:T(8,128)(2,1)S(1)}, u32[]{:S(2)}, u32[]{:S(2)}) async-start(bf16[8,128,256]{2,1,0:T(8,128)(2,1)} %broadcast_select_fusion), calls=%async_computation.1 | async-start | bytes 1048576 | tf_op jit(solution)/shard_map/all_to_all | solution.py:310
  41.4 41.8 %copy-start.1 = (bf16[12,128,256]{2,1,0:T(8,128)(2,1)}, bf16[12,128,256]{2,1,0:T(8,128)(2,1)S(1)}, u32[]{:S(2)}) copy-start(bf16[12,128,256]{2,1,0:T(8,128)(2,1)S(1)} %pad_maximum_fusion.sender_ref) | copy-start | bytes 2359300
  109.6 18.7 %all-to-all-start.2 = ((bf16[8,128,256]{2,1,0:T(8,128)(2,1)}), bf16[8,128,256]{2,1,0:T(8,128)(2,1)S(1)}, u32[]{:S(2)}, u32[]{:S(2)}) async-start(bf16[8,128,256]{2,1,0:T(8,128)(2,1)} %select_reduce_fusion.1), calls=%async_computation.2 | async-start | bytes 1048576 | tf_op jit(solution)/shard_map/all_to_all | solution.py:430
  113.2 75.2 %all-reduce.4.cloned.1.call-start = ((), (), s32[]{:S(2)}) async-start(), calls=%async_computation.3 | async-start | bytes 1048576 | tf_op jit(solution)/shard_map/psum | solution.py:438
  114.8 14.0 %copy-start.14 = (f32[4,128,256]{2,1,0:T(8,128)S(1)}, f32[4,128,256]{2,1,0:T(8,128)}, u32[]{:S(2)}) copy-start(f32[4,128,256]{2,1,0:T(8,128)} %get-tuple-element.30) | copy-start | bytes 1572868
  114.8 14.0 %copy-start.15 = (f32[4,128,256]{2,1,0:T(8,128)S(1)}, f32[4,128,256]{2,1,0:T(8,128)}, u32[]{:S(2)}) copy-start(f32[4,128,256]{2,1,0:T(8,128)} %get-tuple-element.48) | copy-start | bytes 1572868
  129.8 181.6 %all-reduce.6.cloned.1.call-start = ((), (), s32[]{:S(2)}) async-start(), calls=%async_computation.4 | async-start | bytes 262144 | tf_op jit(solution)/shard_map/psum | solution.py:443
Sparse Core Ops, SparseCore 0:
  129.9 33.2 all-reduce.3
  188.5 122.7 all-reduce.5

commit v2 on v1

--- a/solution.py
+++ b/solution.py
@@ -178,8 +178,8 @@
     att_in_ref,
     stats_ref,
     joined_ref,
-    recv_grad_ref,
-    send_grad_ref,
+    node_ref,
+    leaving_ref,
     att_ref,
     grad_ev_ref,
     grad_bias_ref,
@@ -201,7 +201,13 @@
     def _():
         grad_ev_ref[...] = jnp.zeros_like(grad_ev_ref)
         grad_bias_ref[...] = jnp.zeros_like(grad_bias_ref)
-
+        node_ref[...] = jnp.zeros_like(node_ref)
+        leaving_ref[...] = jnp.zeros_like(leaving_ref)
+        att_ref[...] = jnp.zeros_like(att_ref)
+
+    local = local_ref[slot]
+    place = table_ref[slot]
+    own_blocks = node_ref.shape[0]
     right_s[...] = jnp.zeros_like(right_s)
 
     def step_group(group, carry):
@@ -225,7 +231,7 @@
         factor = jnp.sum(
             jnp.where(mask[None], factor_col.reshape(CHUNK, heads, 1), 0.0), axis=1
         )
-        att_ref[0, pl.ds(start, CHUNK), :] = att_in_ref[0, pl.ds(start, CHUNK), :] * factor
+        att_ref[local, pl.ds(start, CHUNK), :] += att_in_ref[0, pl.ds(start, CHUNK), :] * factor
         pair = jnp.concatenate(
             [dlogit.reshape(CHUNK, heads, block), probs.reshape(CHUNK, heads, block)], axis=1
         ).astype(BF16)
@@ -251,15 +257,223 @@
     grad_query = gather_heads(dot(dlogit, keys), heads) * scale
     grad_keys = dot(dlogit, query_wide, 0, 0) * scale
     grad_values = dot(probs_s[...], datt_wide, 0, 0)
-    recv_grad_ref[0] = dot(grad_query.astype(BF16), wq_ref[...], 1, 1) + 0.5 * dot(
+    node_ref[local] += dot(grad_query.astype(BF16), wq_ref[...], 1, 1) + 0.5 * dot(
         left_s[...].astype(BF16), wl_ref[...], 1, 1
     )
-    send_grad_ref[0] = (
+    send_grad = (
         dot(grad_keys.astype(BF16), wk_ref[...], 1, 1)
         + dot(grad_values.astype(BF16), wv_ref[...], 1, 1)
         + 0.5 * dot(right_s[...].astype(BF16), wr_ref[...], 1, 1)
     )
+
+    @pl.when(place < own_blocks)
+    def _():
+        node_ref[place] += send_grad
+
+    @pl.when(place >= own_blocks)
+    def _():
+        leaving_ref[place - own_blocks] = send_grad.astype(BF16)
+
     grad_ev_ref[...] += dot(ctx_s[...], datt_wide, 0, 0)
+
+
+MESH = pl.DeviceIdType.MESH
+
+
+def peers_of(axis, count):
+    me = lax.axis_index(axis)
+    return me, [
+        (offset, lax.rem(me + offset, count), lax.rem(me + count - offset, count))
+        for offset in range(1, count)
+    ]
+
+
+def meet(groups):
+    barrier = pltpu.get_barrier_semaphore()
+    total = 0
+    for axis, peers in groups:
+        for _, target, _ in peers:
+            pl.semaphore_signal(barrier, inc=1, device_id={axis: target}, device_id_type=MESH)
+            total += 1
+    pl.semaphore_wait(barrier, total)
+
+
+def post(axis, peers, sems, source, landing):
+    copies = []
+    for offset, target, _ in peers:
+        copy = pltpu.make_async_remote_copy(
+            src_ref=source(target),
+            dst_ref=landing,
+            send_sem=sems.at[0, offset],
+            recv_sem=sems.at[1, offset],
+            device_id={axis: target},
+            device_id_type=MESH,
+        )
+        copy.start()
+        copies.append(copy)
+    return copies
+
+
+def fetch_kernel(n_recv, wanted_ref, nodes_ref, got_ref, asked_ref, ask_s, reply_s, got_s, ask_sems, reply_sems):
+    me, peers = peers_of("recv", n_recv)
+    meet([("recv", peers)])
+    asks = post("recv", peers, ask_sems, lambda target: wanted_ref.at[target], ask_s.at[me])
+    nodes = nodes_ref[...].astype(F32)
+    for copy in asks:
+        copy.wait_recv()
+    replies = []
+    for peer in peers:
+        offset, target, _ = peer
+        ask = ask_s[target][0:1, :]
+        reply = nodes[0]
+        for at in range(1, nodes.shape[0]):
+            reply = jnp.where(ask == float(at), nodes[at], reply)
+        reply_s[offset] = reply.astype(BF16)
+        replies += post("recv", [peer], reply_sems, lambda target: reply_s.at[offset], got_s.at[me])
+    asked_ref[...] = jnp.zeros_like(asked_ref)
+    got_ref[...] = jnp.zeros_like(got_ref)
+    for _, target, _ in peers:
+        asked_ref[target] = ask_s[target]
+    for copy, (_, _, source) in zip(replies, peers):
+        copy.wait_recv()
+        got_ref[source] = got_s[source]
+    for copy in asks + replies:
+        copy.wait_send()
+
+
+def join_kernel(n_send, stats_ref, joined_ref, all_s, sems):
+    me, peers = peers_of("send", n_send)
+    meet([("send", peers)])
+    copies = post("send", peers, sems, lambda target: stats_ref, all_s.at[me])
+    slots = stats_ref.shape[0]
+    all_s[me] = stats_ref[...]
+    for copy in copies:
+        copy.wait_recv()
+    for slot in range(slots):
+        lands = stats_ref[slot, 3]
+        top = stats_ref[slot, 0]
+        for device in range(n_send):
+            for other in range(slots):
+                top = jnp.maximum(
+                    top,
+                    jnp.where(all_s[device, other, 3] == lands, all_s[device, other, 0], NEG_LARGE),
+                )
+        total = jnp.zeros_like(top)
+        delta = jnp.zeros_like(top)
+        for device in range(n_send):
+            for other in range(slots):
+                part = jnp.where(
+                    all_s[device, other, 3] == lands, jnp.exp(all_s[device, other, 0] - top), 0.0
+                )
+                total = total + part * all_s[device, other, 1]
+                delta = delta + part * all_s[device, other, 2]
+        joined_ref[slot, 0] = top + jnp.log(total)
+        joined_ref[slot, 1] = delta / total
+    for copy in copies:
+        copy.wait_send()
+
+
+def tail_kernel(
+    n_recv,
+    n_send,
+    att_ref,
+    node_ref,
+    leaving_ref,
+    asked_ref,
+    ev_ref,
+    bias_ref,
+    nodes_ref,
+    dout_ref,
+    wo_ref,
+    mixed_ref,
+    grad_ref,
+    bias_out_ref,
+    ev_out_ref,
+    back_s,
+    out_a,
+    in_a,
+    mix_s,
+    small_s,
+    small_all,
+    acc_s,
+    out_n,
+    in_n,
+    fin_s,
+    back_sems,
+    a_sems,
+    mix_sems,
+    small_sems,
+    small_all_sems,
+    n_sems,
+    fin_sems,
+):
+    row, row_peers = peers_of("recv", n_recv)
+    col, col_peers = peers_of("send", n_send)
+    blocks, block, width = node_ref.shape
+    rows = blocks * block
+    share = rows // n_send
+    ev_share = ev_ref.shape[0] // n_send
+    bias_rows = bias_ref.shape[0]
+    meet([("recv", row_peers), ("send", col_peers)])
+    backs = post("recv", row_peers, back_sems, lambda target: leaving_ref.at[target], back_s.at[row])
+    for part in range(n_send):
+        out_a[part, :share] = att_ref[part * share : (part + 1) * share].astype(BF16)
+        out_a[part, share : share + ev_share] = ev_ref[
+            part * ev_share : (part + 1) * ev_share
+        ].astype(BF16)
+        bias = bias_ref[...] if part == 0 else jnp.zeros_like(bias_ref)
+        out_a[part, share + ev_share :] = bias.astype(BF16)
+    sent_a = post("send", col_peers, a_sems, lambda target: out_a.at[target], in_a.at[col])
+    acc_s[...] = node_ref[...].reshape(rows, width)
+    total = out_a[col].astype(F32)
+    for copy, (_, _, source) in zip(sent_a, col_peers):
+        copy.wait_recv()
+        total = total + in_a[source].astype(F32)
+    small_s[row] = total[share:].astype(BF16)
+    smalls = post("recv", row_peers, small_sems, lambda target: small_s.at[row], small_s.at[row])
+    here = pl.ds(pl.multiple_of(col * share, share), share)
+    mixed = nodes_ref[here, :].astype(F32) + dot(total[:share].astype(BF16), wo_ref[...])
+    mix_s[col] = mixed.astype(BF16)
+    mixes = post("send", col_peers, mix_sems, lambda target: mix_s.at[col], mix_s.at[col])
+    for copy, (_, _, source) in zip(backs, row_peers):
+        copy.wait_recv()
+        asked = asked_ref[source][0:1, :]
+        landed = back_s[source].astype(F32)
+        for at in range(blocks):
+            acc_s[at * block : (at + 1) * block, :] += jnp.where(asked == float(at), landed, 0.0)
+    for part in range(n_send):
+        out_n[part] = acc_s[part * share : (part + 1) * share, :].astype(BF16)
+    sent_n = post("send", col_peers, n_sems, lambda target: out_n.at[target], in_n.at[col])
+    for copy in smalls:
+        copy.wait_recv()
+    small = small_s[0].astype(F32)
+    for at in range(1, n_recv):
+        small = small + small_s[at].astype(F32)
+    small_all[col] = small.astype(BF16)
+    small_alls = post(
+        "send", col_peers, small_all_sems, lambda target: small_all.at[col], small_all.at[col]
+    )
+    total = out_n[col].astype(F32)
+    for copy, (_, _, source) in zip(sent_n, col_peers):
+        copy.wait_recv()
+        total = total + in_n[source].astype(F32)
+    fin_s[col] = total.astype(BF16)
+    fins = post("send", col_peers, fin_sems, lambda target: fin_s.at[col], fin_s.at[col])
+    for copy in mixes:
+        copy.wait_recv()
+    mixed_ref[...] = mix_s[...].reshape(rows, width)
+    for copy in small_alls:
+        copy.wait_recv()
+    for part in range(n_send):
+        ev_out_ref[part * ev_share : (part + 1) * ev_share, :] = small_all[part, :ev_share].astype(F32)
+    bias_out_ref[...] = small_all[0, ev_share : ev_share + bias_rows].astype(F32)
+    for copy in fins:
+        copy.wait_recv()
+    for part in range(n_send):
+        span = slice(part * share, (part + 1) * share)
+        grad_ref[span, :] = dout_ref[span, :].astype(F32) + fin_s[part].astype(F32)
+    for copy in backs + sent_a + smalls + mixes + sent_n + small_alls + fins:
+        copy.wait_send()
 
 
 def whole_spec(array):
@@ -296,6 +510,7 @@
     scale = (att_width // heads) ** (-0.5)
     my_recv = lax.axis_index("recv")
     n_recv = lax.axis_size("recv")
+    n_send = lax.axis_size("send")
     base_block = my_recv * nb_local
 
     send_blocks = pairs[1]
@@ -305,11 +520,30 @@
     owner_ids = jnp.arange(n_recv, dtype=jnp.int32)
     hits = (owners[None, :] == owner_ids[:, None]) & remote[None, :]
     wanted = jnp.sum(jnp.where(hits, (send_blocks % nb_local)[None, :], 0), axis=1)
-    requested = lax.all_to_all(wanted, "recv", split_axis=0, concat_axis=0, tiled=True)
     node_blocks = nodes.reshape(nb_local, block, width)
-    got = lax.all_to_all(
-        jnp.take(node_blocks, requested, axis=0), "recv", split_axis=0, concat_axis=0, tiled=True
-    )
+    in_vmem = pl.BlockSpec(memory_space=pltpu.VMEM)
+    asks_shape = (n_recv, 8, width)
+    wants = jnp.broadcast_to(wanted.astype(F32)[:, None, None], asks_shape)
+    got, asked = pl.pallas_call(
+        functools.partial(fetch_kernel, n_recv),
+        in_specs=[in_vmem] * 2,
+        out_specs=[in_vmem] * 2,
+        out_shape=[
+            jax.ShapeDtypeStruct((n_recv, block, width), BF16),
+            jax.ShapeDtypeStruct(asks_shape, F32),
+        ],
+        scratch_shapes=[
+            pltpu.VMEM(asks_shape, F32),
+            pltpu.VMEM((n_recv, block, width), BF16),
+            pltpu.VMEM((n_recv, block, width), BF16),
+            pltpu.SemaphoreType.DMA((2, n_recv)),
+            pltpu.SemaphoreType.DMA((2, n_recv)),
+        ],
+        compiler_params=pltpu.CompilerParams(
+            collective_id=1, has_side_effects=True, vmem_limit_bytes=40 * 2**20
+        ),
+        name="fetch",
+    )(wants, node_blocks)
     table = jnp.concatenate([node_blocks, got], axis=0)
     table_at = jnp.where(remote, nb_local + owners, send_blocks - base_block)
 
@@ -366,18 +600,24 @@
         frame_rows, mask_rows, nodes, d_out, table, *weights,
     )
 
-    all_stats = lax.all_gather(stats, "send").reshape((-1,) + stats.shape[1:])
-    lands = all_stats[:, 3, 0, 0].astype(jnp.int32)
-    here = (lands[None, :] == local_blocks[:, None])[:, :, None, None]
-    tops = all_stats[None, :, 0]
-    top = jnp.max(jnp.where(here, tops, NEG_LARGE), axis=1)
-    shares = jnp.where(here, jnp.exp(tops - top[:, None]), 0.0)
-    total = jnp.sum(shares * all_stats[None, :, 1], axis=1)
-    delta = jnp.sum(shares * all_stats[None, :, 2], axis=1) / total
-    joined = jnp.stack([top + jnp.log(total), delta], axis=1)
+    joined_shape = (slots, 2) + stats.shape[2:]
+    joined = pl.pallas_call(
+        functools.partial(join_kernel, n_send),
+        in_specs=[in_vmem],
+        out_specs=in_vmem,
+        out_shape=jax.ShapeDtypeStruct(joined_shape, F32),
+        scratch_shapes=[
+            pltpu.VMEM((n_send,) + stats.shape, F32),
+            pltpu.SemaphoreType.DMA((2, n_send)),
+        ],
+        compiler_params=pltpu.CompilerParams(collective_id=2, has_side_effects=True),
+        name="join",
+    )(stats)
 
     weights = (w_query, w_key, w_value, w_left, w_right, w_out)
-    grad_shape = (slots, block, width)
+    node_shape = (nb_local, block, width)
+    away_shape = (n_recv, block, width)
+    att_sum_shape = (nb_local, block, att_width)
     backward = pl.pallas_call(
         functools.partial(backward_kernel, scale),
         grid_spec=pltpu.PrefetchScalarGridSpec(
@@ -393,9 +633,9 @@
                 )
             ],
             out_specs=[
-                slot_spec(grad_shape),
-                slot_spec(grad_shape),
-                slot_spec(att_shape),
+                whole_spec(node_blocks),
+                whole_spec(got),
+                whole_spec(jax.ShapeDtypeStruct(att_sum_shape, F32)),
                 whole_spec(w_edge_value),
                 whole_spec(w_bias),
             ],
@@ -408,39 +648,60 @@
             ],
         ),
         out_shape=[
-            jax.ShapeDtypeStruct(grad_shape, F32),
-            jax.ShapeDtypeStruct(grad_shape, F32),
-            jax.ShapeDtypeStruct(att_shape, F32),
+            jax.ShapeDtypeStruct(node_shape, F32),
+            jax.ShapeDtypeStruct(away_shape, BF16),
+            jax.ShapeDtypeStruct(att_sum_shape, F32),
             jax.ShapeDtypeStruct(w_edge_value.shape, F32),
             jax.ShapeDtypeStruct(w_bias.shape, F32),
         ],
         compiler_params=pltpu.CompilerParams(vmem_limit_bytes=50 * 2**20),
         name="backward",
     )
-    recv_grads, send_grads, att, grad_ev, grad_bias = backward(
+    node_sum, leaving, att, grad_ev, grad_bias = backward(
         local_blocks, table_at, mask_rows, nodes, d_out, table, *weights,
         logits, dprobs, slopes, sums, wides, att_parts, stats, joined,
     )
 
-    block_ids = jnp.arange(nb_local, dtype=jnp.int32)
-    to_recv = (local_blocks[None, :] == block_ids[:, None])[:, :, None, None]
-    own = (~remote & ((send_blocks - base_block)[None, :] == block_ids[:, None]))[:, :, None, None]
-    away = hits[:, :, None, None]
-    leaving = jnp.sum(jnp.where(away, send_grads[None], 0.0), axis=1).astype(BF16)
-    back = lax.all_to_all(leaving, "recv", split_axis=0, concat_axis=0, tiled=True)
-    landing = (requested[None, :] == block_ids[:, None])[:, :, None, None]
-    node_part = (
-        jnp.sum(jnp.where(to_recv, recv_grads[None], 0.0), axis=1)
-        + jnp.sum(jnp.where(own, send_grads[None], 0.0), axis=1)
-        + jnp.sum(jnp.where(landing, back[None].astype(F32), 0.0), axis=1)
-    ).reshape(rows, width)
-    att_part = jnp.sum(jnp.where(to_recv, att[None], 0.0), axis=1).reshape(rows, att_width)
-    attended, node_grad = lax.psum((att_part, node_part), "send")
-    mixed = (
-        nodes.astype(F32) + jnp.dot(attended.astype(BF16), w_out, preferred_element_type=F32)
-    ).astype(BF16)
-    grad_nodes = d_out.astype(F32) + node_grad
-    grad_bias, grad_ev = lax.psum((grad_bias, grad_ev), ("recv", "send"))
+    share = rows // n_send
+    ev_share = edge_width // n_send
+    bias_rows = heads * edge_width // att_width
+    bias_flat = jnp.pad(grad_bias.reshape(bias_rows, att_width), ((0, 16 - bias_rows), (0, 0)))
+    tail_rows = ev_share + 16
+    mixed, grad_nodes, bias_flat, grad_ev = pl.pallas_call(
+        functools.partial(tail_kernel, n_recv, n_send),
+        in_specs=[in_vmem] * 9,
+        out_specs=[in_vmem] * 4,
+        out_shape=[
+            jax.ShapeDtypeStruct((rows, width), BF16),
+            jax.ShapeDtypeStruct((rows, width), F32),
+            jax.ShapeDtypeStruct((16, att_width), F32),
+            jax.ShapeDtypeStruct((edge_width, att_width), F32),
+        ],
+        scratch_shapes=[
+            pltpu.VMEM(away_shape, BF16),
+            pltpu.VMEM((n_send, share + tail_rows, att_width), BF16),
+            pltpu.VMEM((n_send, share + tail_rows, att_width), BF16),
+            pltpu.VMEM((n_send, share, width), BF16),
+            pltpu.VMEM((n_recv, tail_rows, att_width), BF16),
+            pltpu.VMEM((n_send, tail_rows, att_width), BF16),
+            pltpu.VMEM((rows, width), F32),
+            pltpu.VMEM((n_send, share, width), BF16),
+            pltpu.VMEM((n_send, share, width), BF16),
+            pltpu.VMEM((n_send, share, width), BF16),
+            pltpu.SemaphoreType.DMA((2, n_recv)),
+            pltpu.SemaphoreType.DMA((2, n_send)),
+            pltpu.SemaphoreType.DMA((2, n_send)),
+            pltpu.SemaphoreType.DMA((2, n_recv)),
+            pltpu.SemaphoreType.DMA((2, n_send)),
+            pltpu.SemaphoreType.DMA((2, n_send)),
+            pltpu.SemaphoreType.DMA((2, n_send)),
+        ],
+        compiler_params=pltpu.CompilerParams(
+            collective_id=3, has_side_effects=True, vmem_limit_bytes=40 * 2**20
+        ),
+        name="tail",
+    )(att.reshape(rows, att_width), node_sum, leaving, asked, grad_ev, bias_flat, nodes, d_out, w_out)
+    grad_bias = bias_flat[:bias_rows].reshape(heads, edge_width)
     return (mixed, grad_nodes, grad_bias, grad_ev)
 
 

time: 320 us -> 139 us (0.43)
  waiting for transfers between devices: 148 us -> 0 us
  blocking collectives: 76.9 us -> 0 us
  Pallas kernels: 60.1 us -> 114 us
  local copies, waits for them, and re-layouts: 3.39 us -> 21.8 us
  between operations: 14.4 us -> 0.88 us
  other arithmetic: 9.1 us -> 1.64 us
  starting transfers between devices: 7.24 us -> 0 us
    psum x2 -> x0, waiting for transfers between devices: 121 us -> none  [the longest x1 121 us: body(): grad_bias, grad_ev = lax.psum((grad_bias, grad_ev), ('recv', 'send'))]
    psum x2 -> x0, blocking collectives: 57.6 us -> none  [the longest x1 38.3 us: body(): grad_bias, grad_ev = lax.psum((grad_bias, grad_ev), ('recv', 'send'))]
    pallas_call x0 -> x3, Pallas kernels: none -> 53.3 us  [the longest x1 26.8 us: body(): pl.pallas_call(functools.partial(tail_kernel, n_recv, n_send), in_specs=[...]
    all_to_all x2 -> x0, waiting for transfers between devices: 26.5 us -> none  [the longest x1 13.4 us: body(): lax.all_to_all(leaving, 'recv', split_axis=0, concat_axis=0, tiled=True)]
    unnamed x35 -> x69, local copies, waits for them, and re-layouts: 1.66 us -> 20.4 us
    all_to_all x1 -> x0, blocking collectives: 13.5 us -> none  [body(): lax.all_to_all(wanted, 'recv', split_axis=0, concat_axis=0, tiled=True)]
    all_to_all x2 -> x0, starting transfers between devices: 7.16 us -> none  [the longest x1 3.66 us: body(): lax.all_to_all(leaving, 'recv', split_axis=0, concat_axis=0, tiled=True)]
    all_gather x1 -> x0, blocking collectives: 5.77 us -> none  [body(): all_stats = lax.all_gather(stats, 'send').reshape((-1,) + stats.shape[1:])]
  transfers between devices with their start and end apart: 4 -> 0, of which waited for: 3 -> 0; matrix products, arithmetic and copies ran while one was open for 1% -> 0% of each run, Pallas kernels for 0% -> 0%
where the time goes in v2:
time: 139 us; the launch traced here: 138 us
  Pallas kernels  114 us (82%)
  local copies, waits for them, and re-layouts  21.8 us (16%)
  other arithmetic  1.64 us (1%)
    pallas_call x1, Pallas kernels, body(): forward(local_blocks, table_at, pairs[0], send_blocks, frames, frame_rows...  35.1 us
    pallas_call x1, Pallas kernels, body(): pl.pallas_call(functools.partial(tail_kernel, n_recv, n_send), in_specs=[...  26.8 us
    pallas_call x1, Pallas kernels, body(): backward(local_blocks, table_at, mask_rows, nodes, d_out, table, *weights...  25.3 us
    unnamed x69, local copies, waits for them, and re-layouts  20.4 us
    pallas_call x1, Pallas kernels, body(): pl.pallas_call(functools.partial(fetch_kernel, n_recv), in_specs=[in_vmem...  20 us
    pallas_call x1, Pallas kernels, body(): pl.pallas_call(functools.partial(join_kernel, n_send), in_specs=[in_vmem]...  6.54 us

profile of v2, /device:TPU:0, one launch (start us, length us, event | category | flops | bytes accessed | tf_op | source)
XLA Modules:
  0.0 138.0 jit_solution(15425240830090890193)
XLA Ops:
  0.6 0.0 copy-start.17
  0.6 0.0 copy-start.30
  0.7 0.8 compare_select_fusion
  1.4 0.7 compare_bitcast_fusion
  2.1 0.1 select_reduce_fusion
  2.2 0.8 slice_bitcast_fusion.1
  3.0 0.1 broadcast_in_dim.27.wanted_ref
  3.1 1.0 copy-done.1
  4.0 0.0 copy-start.11
  4.0 0.0 copy-start.13
  4.1 0.0 copy-start.19
  4.1 20.0 %fetch.1 = (bf16[8,128,256]{2,1,0:T(8,128)(2,1)S(1)}, f32[8,8,256]{2,1,0:T(8,128)S(1)}) custom-call(f32[8,8,256]{2,1,0:T(8,128)S(1)} %broadcast_in_dim.27.wanted_ref, bf16[4,128,256]{2,1,0:T(8,128)(2,1)S(1)} %bitcast.18), custom_call_target="tpu_custom_call" | custom-call | tf_op jit(solution)/shard_map/fetch/pallas_call | solution.py:527
  24.1 0.0 copy-start.27
  24.1 0.1 pad_maximum_fusion.sender_ref
  24.1 0.0 copy-start.2
  24.2 0.9 copy-done.2
  25.1 0.9 copy-done.4
  26.1 0.9 copy-done.6
  27.0 0.9 copy-done.8
  27.9 0.9 copy-done.10
  28.8 0.9 copy-done.12
  29.7 0.8 copy-done.16
  30.5 0.8 copy-done.18
  31.4 0.7 copy-done.25
  32.1 0.8 copy-done.26
  32.9 0.7 copy-done.29
  33.6 0.7 copy-done.31
  34.3 0.7 copy-done.32
  34.9 35.1 %forward.1 = (f32[4,128,8,128]{3,2,1,0:T(8,128)}, f32[4,128,8,128]{3,2,1,0:T(8,128)}, bf16[4,128,128,128]{3,2,1,0:T(8,128)(2,1)}, bf16[4,128,16,128]{3,2,1,0:T(8...) custom-call(s32[4]{0:T(128)S(1)} %get-tuple-element.46.local_ref, ...), custom_call_target="tpu_custom_call" | custom-call | tf_op jit(solution)/shard_map/forward/pallas_call | solution.py:598
  70.1 0.8 copy-done.14
  70.9 0.6 copy-done.20
  71.5 0.0 copy-done.27
  71.5 6.5 %join.1.joined_ref = f32[4,2,8,128]{3,2,1,0:T(8,128)} custom-call(f32[4,4,8,128]{3,2,1,0:T(8,128)} %copy-done.20), custom_call_target="tpu_custom_call" | custom-call | tf_op jit(solution)/shard_map/join/pallas_call | solution.py:604
  78.0 0.0 copy-done
  78.1 0.0 copy-start.15
  78.1 1.0 copy-done.15
  79.2 0.8 copy-done.21
  80.0 0.8 copy-done.22
  80.8 25.3 %backward.1 = (f32[4,128,256]{2,1,0:T(8,128)S(1)}, bf16[8,128,256]{2,1,0:T(8,128)(2,1)S(1)}, f32[4,128,256]{2,1,0:T(8,128)S(1)}, f32[128,256]{1,0:T(8,128)S(1)}, f32[8,128]{1,0:T(8,128)S(1)}) custom-call(s32[4]{0:T(128)S(1)} %get-tuple-element.46.local_ref, s32[4]{0:T(128)S(1)} %get-tuple-element.45.table_ref, s32[4,1,128]{2,1,0:T(1,128)S(1)} %bitcast.23, ...), custom_call_target="tpu_custom_call" | custom-call | tf_op jit(solution)/shard_map/backward/pallas_call | solution.py:660
  106.0 0.0 copy-start.23
  106.1 0.6 copy-done.23
  106.7 0.9 copy-done.24
  107.6 0.8 copy-done.28
  108.5 26.8 %tail.1 = (bf16[512,256]{1,0:T(8,128)(2,1)S(1)}, f32[512,256]{1,0:T(8,128)S(1)}, f32[16,256]{1,0:T(8,128)S(1)}, f32[128,256]{1,0:T(8,128)S(1)}) custom-call(f32[512,256]{1,0:T(8,128)S(1)} %bitcast.20, f32[4,128,256]{2,1,0:T(8,128)S(1)} %get-tuple-element.31.node_ref, bf16[8,128,256]{2,1,0:T(8,128)(2,1)S(1)} %get-tuple-element.32.leaving_ref, ...), custom_call_target="tpu_custom_call" | custom-call | tf_op jit(solution)/shard_map/tail/pallas_call | solution.py:670
  135.2 0.6 reshape.38
  135.8 0.7 copy.21
  136.5 0.8 copy.22
  137.3 0.7 copy.23
  (38 shorter events, 0.1 us)
Async XLA Ops:
  0.6 77.4 %copy-start.17 = (bf16[256,128]{1,0:T(8,128)(2,1)S(1)}, bf16[256,128]{1,0:T(8,128)(2,1)}, u32[]{:S(2)}) copy-start(bf16[256,128]{1,0:T(8,128)(2,1)} %wl_ref.3) | copy-start | bytes 196612
  0.6 77.4 %copy-start.30 = (s32[4,128]{1,0:T(4,128)S(1)}, s32[4,128]{1,0:T(4,128)}, u32[]{:S(2)}) copy-start(s32[4,128]{1,0:T(4,128)} %param.17) | copy-start | bytes 6148
  3.1 1.0 copy-start.1
  4.0 74.0 %copy-start.3 = (bf16[512,256]{1,0:T(8,128)(2,1)S(1)}, bf16[512,256]{1,0:T(8,128)(2,1)}, u32[]{:S(2)}) copy-start(bf16[512,256]{1,0:T(8,128)(2,1)} %nodes_ref.5) | copy-start | bytes 786436
  4.0 74.1 %copy-start.5 = (bf16[512,256]{1,0:T(8,128)(2,1)S(1)}, bf16[512,256]{1,0:T(8,128)(2,1)}, u32[]{:S(2)}) copy-start(bf16[512,256]{1,0:T(8,128)(2,1)} %dout_ref.5) | copy-start | bytes 786436
  4.0 74.1 %copy-start.7 = (bf16[256,256]{1,0:T(8,128)(2,1)S(1)}, bf16[256,256]{1,0:T(8,128)(2,1)}, u32[]{:S(2)}) copy-start(bf16[256,256]{1,0:T(8,128)(2,1)} %wo_ref.5) | copy-start | bytes 393220
  4.0 74.1 %copy-start.9 = (bf16[256,256]{1,0:T(8,128)(2,1)S(1)}, bf16[256,256]{1,0:T(8,128)(2,1)}, u32[]{:S(2)}) copy-start(bf16[256,256]{1,0:T(8,128)(2,1)} %wq_ref.3) | copy-start | bytes 393220
  4.0 74.1 %copy-start.11 = (bf16[256,256]{1,0:T(8,128)(2,1)S(1)}, bf16[256,256]{1,0:T(8,128)(2,1)}, u32[]{:S(2)}) copy-start(bf16[256,256]{1,0:T(8,128)(2,1)} %wk_ref.3) | copy-start | bytes 393220
  4.0 74.1 %copy-start.13 = (bf16[256,256]{1,0:T(8,128)(2,1)S(1)}, bf16[256,256]{1,0:T(8,128)(2,1)}, u32[]{:S(2)}) copy-start(bf16[256,256]{1,0:T(8,128)(2,1)} %wv_ref.3) | copy-start | bytes 393220
  4.1 74.1 %copy-start.19 = (bf16[256,128]{1,0:T(8,128)(2,1)S(1)}, bf16[256,128]{1,0:T(8,128)(2,1)}, u32[]{:S(2)}) copy-start(bf16[256,128]{1,0:T(8,128)(2,1)} %wr_ref.3) | copy-start | bytes 196612
  24.1 47.4 %copy-start.27 = (f32[8,8,256]{2,1,0:T(8,128)}, f32[8,8,256]{2,1,0:T(8,128)S(1)}, u32[]{:S(2)}) copy-start(f32[8,8,256]{2,1,0:T(8,128)S(1)} %get-tuple-element.33.asked_ref) | copy-start | bytes 196612
  24.1 1.0 copy-start.2
  25.1 0.9 copy-start.4
  26.1 0.9 copy-start.6
  27.0 0.9 copy-start.8
  27.9 0.9 copy-start.10
  28.8 0.9 copy-start.12
  29.7 0.8 copy-start.16
  30.5 0.8 copy-start.18
  31.3 0.7 copy-start.25
  32.1 0.8 copy-start.26
  32.9 0.7 copy-start.29
  33.6 0.7 copy-start.31
  34.3 0.7 copy-start.32
  34.9 43.1 %copy-start = (bf16[12,128,256]{2,1,0:T(8,128)(2,1)}, bf16[12,128,256]{2,1,0:T(8,128)(2,1)S(1)}, u32[]{:S(2)}) copy-start(bf16[12,128,256]{2,1,0:T(8,128)(2,1)S(1)} %pad_maximum_fusion.sender_ref) | copy-start | bytes 2359300
  70.1 0.8 copy-start.14
  70.9 0.6 copy-start.20
  78.1 1.0 copy-start.15
  79.2 0.8 copy-start.21
  80.0 0.8 copy-start.22
  106.0 0.7 copy-start.23
  106.7 0.9 copy-start.24
  107.6 0.8 copy-start.28

commit v3 on v2

--- a/solution.py
+++ b/solution.py
@@ -9,6 +9,7 @@
 
 NEG_LARGE = -1e30
 CHUNK = 16
+VMEM_LIMIT = 60 * 2**20
 F32 = jnp.float32
 BF16 = jnp.bfloat16
 
@@ -92,15 +93,16 @@
     nodes = nodes_ref[...]
     sender = sender_ref[0]
     query = dot(nodes, wq_ref[...]).astype(BF16)
-    left_s[...] = dot(nodes, wl_ref[...]).astype(BF16).astype(F32) * 0.5
+    left_s[...] = dot(nodes, wl_ref[...]) * 0.5
     datt = dot(dout_ref[...], wo_ref[...], 1, 1).astype(BF16)
     keys = dot(sender, wk_ref[...]).astype(BF16)
     values = dot(sender, wv_ref[...]).astype(BF16)
-    right = dot(sender, wr_ref[...]).astype(BF16).astype(F32) * 0.5
-    right_same = right + fe_ref[...].astype(F32) * 0.5
+    right = dot(sender, wr_ref[...]) * 0.5
+    right_same = (right + fe_ref[...].astype(F32) * 0.5).astype(BF16)
+    right = right.astype(BF16)
     frame_col = jnp.broadcast_to(
         to_column(frame_row_ref[0].astype(F32)), (block, edge_width)
-    )
+    ).astype(BF16)
     datt_wide = spread(datt, heads)
     logit_ref[0] = (dot(spread(query, heads), keys, 1, 1) * scale).reshape(block, heads, block)
     dprob_ref[0] = dot(datt_wide, values, 1, 1).reshape(block, heads, block)
@@ -109,17 +111,20 @@
     wide_ref[0] = jnp.concatenate([bias, dctx], axis=1).astype(BF16)
     recv_start = recv_ref[slot] * block
 
+    one = jnp.ones((), BF16)
+
     def edge_step(group, carry):
         start = group * CHUNK
         left_rows = left_s[pl.ds(start, CHUNK), :]
         for step in range(CHUNK):
             at = start + step
-            frame = frames_ref[recv_start + at].astype(F32)
-            half = left_rows[step : step + 1] + jnp.where(frame_col == frame, right_same, right)
+            frame = frames_ref[recv_start + at].astype(F32).astype(BF16)
+            left = left_rows[step : step + 1].astype(BF16)
+            half = left + jnp.where(frame_col == frame, right_same, right)
             turn = jnp.tanh(half)
             gain = half * turn
-            edge = (half + gain).astype(BF16)
-            slope_ref[0, at] = ((1.0 + turn) * (1.0 + half - gain)).astype(BF16)
+            edge = half + gain
+            slope_ref[0, at] = (one + turn) * (one + (half - gain))
             edge_s[at] = edge
             both = dot(wide_ref[0, at], edge, 1, 1)
             logit_ref[0, at] = logit_ref[0, at] + both[:heads]
@@ -314,17 +319,26 @@
     return copies
 
 
-def fetch_kernel(n_recv, wanted_ref, nodes_ref, got_ref, asked_ref, ask_s, reply_s, got_s, ask_sems, reply_sems):
+def fetch_kernel(
+    n_recv, pairs_ref, nodes_ref, got_ref, asked_ref, want_s, ask_s, reply_s, got_s, ask_sems, reply_sems
+):
     me, peers = peers_of("recv", n_recv)
+    blocks = nodes_ref.shape[0]
+    for _, target, _ in peers:
+        wanted = 0
+        for slot in range(pairs_ref.shape[1]):
+            sender = pairs_ref[1, slot]
+            wanted = wanted + jnp.where(sender // blocks == target, sender % blocks, 0)
+        want_s[target] = jnp.full(want_s.shape[1:], wanted, jnp.int32).astype(F32)
     meet([("recv", peers)])
-    asks = post("recv", peers, ask_sems, lambda target: wanted_ref.at[target], ask_s.at[me])
+    asks = post("recv", peers, ask_sems, lambda target: want_s.at[target], ask_s.at[me])
     nodes = nodes_ref[...].astype(F32)
     for copy in asks:
         copy.wait_recv()
     replies = []
     for peer in peers:
         offset, target, _ = peer
-        ask = ask_s[target][0:1, :]
+        ask = ask_s[target][0:1, 0:1]
         reply = nodes[0]
         for at in range(1, nodes.shape[0]):
             reply = jnp.where(ask == float(at), nodes[at], reply)
@@ -437,7 +451,7 @@
     mixes = post("send", col_peers, mix_sems, lambda target: mix_s.at[col], mix_s.at[col])
     for copy, (_, _, source) in zip(backs, row_peers):
         copy.wait_recv()
-        asked = asked_ref[source][0:1, :]
+        asked = asked_ref[source][0:1, 0:1]
         landed = back_s[source].astype(F32)
         for at in range(blocks):
             acc_s[at * block : (at + 1) * block, :] += jnp.where(asked == float(at), landed, 0.0)
@@ -518,15 +532,12 @@
     owners = send_blocks // nb_local
     remote = owners != my_recv
     owner_ids = jnp.arange(n_recv, dtype=jnp.int32)
-    hits = (owners[None, :] == owner_ids[:, None]) & remote[None, :]
-    wanted = jnp.sum(jnp.where(hits, (send_blocks % nb_local)[None, :], 0), axis=1)
     node_blocks = nodes.reshape(nb_local, block, width)
     in_vmem = pl.BlockSpec(memory_space=pltpu.VMEM)
-    asks_shape = (n_recv, 8, width)
-    wants = jnp.broadcast_to(wanted.astype(F32)[:, None, None], asks_shape)
+    asks_shape = (n_recv, 8, 128)
     got, asked = pl.pallas_call(
         functools.partial(fetch_kernel, n_recv),
-        in_specs=[in_vmem] * 2,
+        in_specs=[pl.BlockSpec(memory_space=pltpu.SMEM), in_vmem],
         out_specs=[in_vmem] * 2,
         out_shape=[
             jax.ShapeDtypeStruct((n_recv, block, width), BF16),
@@ -534,16 +545,17 @@
         ],
         scratch_shapes=[
             pltpu.VMEM(asks_shape, F32),
+            pltpu.VMEM(asks_shape, F32),
             pltpu.VMEM((n_recv, block, width), BF16),
             pltpu.VMEM((n_recv, block, width), BF16),
             pltpu.SemaphoreType.DMA((2, n_recv)),
             pltpu.SemaphoreType.DMA((2, n_recv)),
         ],
         compiler_params=pltpu.CompilerParams(
-            collective_id=1, has_side_effects=True, vmem_limit_bytes=40 * 2**20
+            collective_id=1, has_side_effects=True, vmem_limit_bytes=VMEM_LIMIT
         ),
         name="fetch",
-    )(wants, node_blocks)
+    )(pairs, node_blocks)
     table = jnp.concatenate([node_blocks, got], axis=0)
     table_at = jnp.where(remote, nb_local + owners, send_blocks - base_block)
 
@@ -592,7 +604,7 @@
             jax.ShapeDtypeStruct(att_shape, F32),
             jax.ShapeDtypeStruct(stats_shape, F32),
         ],
-        compiler_params=pltpu.CompilerParams(vmem_limit_bytes=50 * 2**20),
+        compiler_params=pltpu.CompilerParams(vmem_limit_bytes=VMEM_LIMIT),
         name="forward",
     )
     logits, dprobs, slopes, sums, wides, att_parts, stats = forward(
@@ -610,7 +622,9 @@
             pltpu.VMEM((n_send,) + stats.shape, F32),
             pltpu.SemaphoreType.DMA((2, n_send)),
         ],
-        compiler_params=pltpu.CompilerParams(collective_id=2, has_side_effects=True),
+        compiler_params=pltpu.CompilerParams(
+            collective_id=2, has_side_effects=True, vmem_limit_bytes=VMEM_LIMIT
+        ),
         name="join",
     )(stats)
 
@@ -654,7 +668,7 @@
             jax.ShapeDtypeStruct(w_edge_value.shape, F32),
             jax.ShapeDtypeStruct(w_bias.shape, F32),
         ],
-        compiler_params=pltpu.CompilerParams(vmem_limit_bytes=50 * 2**20),
+        compiler_params=pltpu.CompilerParams(vmem_limit_bytes=VMEM_LIMIT),
         name="backward",
     )
     node_sum, leaving, att, grad_ev, grad_bias = backward(
@@ -697,7 +711,7 @@
             pltpu.SemaphoreType.DMA((2, n_send)),
         ],
         compiler_params=pltpu.CompilerParams(
-            collective_id=3, has_side_effects=True, vmem_limit_bytes=40 * 2**20
+            collective_id=3, has_side_effects=True, vmem_limit_bytes=VMEM_LIMIT
         ),
         name="tail",
     )(att.reshape(rows, att_width), node_sum, leaving, asked, grad_ev, bias_flat, nodes, d_out, w_out)

time: 139 us -> 133 us (0.957)
  local copies, waits for them, and re-layouts: 21.8 us -> 8.98 us
  Pallas kernels: 114 us -> 119 us
  other arithmetic: 1.64 us -> 3.47 us
    unnamed x69 -> x3, local copies, waits for them, and re-layouts: 20.4 us -> 5.1 us
    pallas_call x1, Pallas kernels: 26.8 us -> 29.5 us  [body(): pl.pallas_call(functools.partial(tail_kernel, n_recv, n_send), in_specs=[...]
    concatenate x1, other arithmetic: 0.07 us -> 2.11 us  [body(): table = jnp.concatenate([node_blocks, got], axis=0)]
    pallas_call x1, Pallas kernels: 25.3 us -> 27.1 us  [body(): backward(local_blocks, table_at, mask_rows, nodes, d_out, table, *weights...]
    pallas_call x1, Pallas kernels: 20 us -> 21.6 us  [body(): pl.pallas_call(functools.partial(fetch_kernel, n_recv), in_specs=[pl.Bloc...]
where the time goes in v3:
time: 133 us; the launch traced here: 132 us
  Pallas kernels  119 us (89%)
  local copies, waits for them, and re-layouts  8.98 us (7%)
  other arithmetic  3.47 us (3%)
    pallas_call x1, Pallas kernels, body(): forward(local_blocks, table_at, pairs[0], send_blocks, frames, frame_rows...  33.8 us
    pallas_call x1, Pallas kernels, body(): pl.pallas_call(functools.partial(tail_kernel, n_recv, n_send), in_specs=[...  29.5 us
    pallas_call x1, Pallas kernels, body(): backward(local_blocks, table_at, mask_rows, nodes, d_out, table, *weights...  27.1 us
    pallas_call x1, Pallas kernels, body(): pl.pallas_call(functools.partial(fetch_kernel, n_recv), in_specs=[pl.Bloc...  21.6 us
    pallas_call x1, Pallas kernels, body(): pl.pallas_call(functools.partial(join_kernel, n_send), in_specs=[in_vmem]...  6.54 us
    unnamed x3, local copies, waits for them, and re-layouts  5.1 us

profile of v3, /device:TPU:0, one launch (start us, length us, event | category | flops | bytes accessed | tf_op | source)
XLA Modules:
  0.0 131.7 jit_solution(10660705938096992756)
XLA Ops:
  0.6 1.4 %compare_select_fusion = (s32[4]{0:T(128)}, s32[4]{0:T(128)}) fusion(s32[]{:T(128)S(6)} %axis_index.15, s32[]{:T(128)S(6)} %mul.3, s32[2,4]{1,0:T(2,128)} %pairs_ref.1), kind=kLoop, calls=%fused_computation.1 | loop fusion | flops 80 | bytes 72 | tf_op jit(solution)/shard_map/jit(_where)/select_n | solution.py:560
  2.0 1.3 slice_bitcast_fusion
  3.3 21.6 %fetch.1 = (bf16[8,128,256]{2,1,0:T(8,128)(2,1)}, f32[8,8,128]{2,1,0:T(8,128)}) custom-call(s32[2,4]{1,0:T(2,128)} %pairs_ref.1, bf16[4,128,256]{2,1,0:T(8,128)(2,1)} %bitcast.13), custom_call_target="tpu_custom_call" | custom-call | tf_op jit(solution)/shard_map/fetch/pallas_call | solution.py:538
  24.9 2.1 %pad_maximum_fusion.sender_ref = bf16[12,128,256]{2,1,0:T(8,128)(2,1)} fusion(bf16[8,128,256]{2,1,0:T(8,128)(2,1)} %get-tuple-element.22, bf16[4,128,256]{2,1,0:T(8,128)(2,1)} %bitcast.14), kind=kLoop, calls=%fused_computation | loop fusion | flops 393216 | bytes 1572864 | tf_op jit(solution)/shard_map/concatenate | solution.py:559
  27.0 33.8 %forward.1 = (f32[4,128,8,128]{3,2,1,0:T(8,128)}, f32[4,128,8,128]{3,2,1,0:T(8,128)}, bf16[4,128,128,128]{3,2,1,0:T(8,128)(2,1)}, bf16[4,128,16,128]{3,2,1,0:T(8...) custom-call(s32[4]{0:T(128)} %get-tuple-element.43.local_ref, ...), custom_call_target="tpu_custom_call" | custom-call | tf_op jit(solution)/shard_map/forward/pallas_call | solution.py:610
  60.8 6.5 %join.1.joined_ref = f32[4,2,8,128]{3,2,1,0:T(8,128)} custom-call(f32[4,4,8,128]{3,2,1,0:T(8,128)} %get-tuple-element.29.stats_ref), custom_call_target="tpu_custom_call" | custom-call | tf_op jit(solution)/shard_map/join/pallas_call | solution.py:616
  67.4 27.1 %backward.1 = (f32[4,128,256]{2,1,0:T(8,128)}, bf16[8,128,256]{2,1,0:T(8,128)(2,1)}, f32[4,128,256]{2,1,0:T(8,128)}, f32[128,256]{1,0:T(8,128)}, f32[8,128]{1,0:T(8,128)}) custom-call(s32[4]{0:T(128)} %get-tuple-element.43.local_ref, s32[4]{0:T(128)} %get-tuple-element.42.table_ref, s32[4,1,128]{2,1,0:T(1,128)} %bitcast.18, bf16[512,256]{1,0:T(8,128)(2,1)} %nodes_ref.5, ...), custom_call_target="tpu_custom_call" | custom-call | tf_op jit(solution)/shard_map/backward/pallas_call | solution.py:674
  94.5 0.7 reshape.34
  95.2 0.6 pad.4.bias_ref
  95.8 29.5 %tail.1 = (bf16[512,256]{1,0:T(8,128)(2,1)}, f32[512,256]{1,0:T(8,128)}, f32[16,256]{1,0:T(8,128)}, f32[128,256]{1,0:T(8,128)}) custom-call(f32[512,256]{1,0:T(8,128)} %bitcast.15, f32[4,128,256]{2,1,0:T(8,128)} %get-tuple-element.31.node_ref, bf16[8,128,256]{2,1,0:T(8,128)(2,1)} %get-tuple-element.32.leaving_ref, f32[8,8,128]{2,1,0:T(8,128)} %get-tuple-element.33.asked_ref, ...), custom_call_target="tpu_custom_call" | custom-call | tf_op jit(solution)/shard_map/tail/pallas_call | solution.py:684
  125.3 0.7 slice.12
  126.0 0.6 reshape.35
  126.6 1.7 %copy.21 = bf16[512,256]{1,0:T(8,128)(2,1)} copy(bf16[512,256]{1,0:T(8,128)(2,1)} %get-tuple-element.48) | data formatting | bytes 524288
  128.2 1.9 %copy.22 = f32[512,256]{1,0:T(8,128)} copy(f32[512,256]{1,0:T(8,128)} %get-tuple-element.49) | data formatting | bytes 1048576
  130.1 1.6 %copy.23 = f32[128,256]{1,0:T(8,128)} copy(f32[128,256]{1,0:T(8,128)} %get-tuple-element.51) | data formatting | bytes 262144

commit v4 on v3

--- a/solution.py
+++ b/solution.py
@@ -9,7 +9,10 @@
 
 NEG_LARGE = -1e30
 CHUNK = 16
+GROUP = 8
+BIAS_ROWS = 16
 VMEM_LIMIT = 60 * 2**20
+TAIL_LIMIT = 32 * 2**20
 F32 = jnp.float32
 BF16 = jnp.bfloat16
 
@@ -57,10 +60,8 @@
 
 def forward_kernel(
     scale,
-    local_ref,
-    table_ref,
-    recv_ref,
-    send_ref,
+    own_blocks,
+    pairs_ref,
     frames_ref,
     frame_row_ref,
     mask_ref,
@@ -109,26 +110,31 @@
     dctx = dot(datt_wide, wev_ref[...], 1, 1).reshape(block, heads, edge_width)
     bias = jnp.broadcast_to(wb_ref[...].astype(F32)[None], dctx.shape)
     wide_ref[0] = jnp.concatenate([bias, dctx], axis=1).astype(BF16)
-    recv_start = recv_ref[slot] * block
+    recv_start = pairs_ref[0, slot] * block
 
     one = jnp.ones((), BF16)
 
     def edge_step(group, carry):
         start = group * CHUNK
-        left_rows = left_s[pl.ds(start, CHUNK), :]
-        for step in range(CHUNK):
-            at = start + step
-            frame = frames_ref[recv_start + at].astype(F32).astype(BF16)
-            left = left_rows[step : step + 1].astype(BF16)
-            half = left + jnp.where(frame_col == frame, right_same, right)
-            turn = jnp.tanh(half)
-            gain = half * turn
-            edge = half + gain
-            slope_ref[0, at] = (one + turn) * (one + (half - gain))
-            edge_s[at] = edge
-            both = dot(wide_ref[0, at], edge, 1, 1)
-            logit_ref[0, at] = logit_ref[0, at] + both[:heads]
-            dprob_ref[0, at] = dprob_ref[0, at] + both[heads:]
+        left_rows = left_s[pl.ds(start, CHUNK), :].astype(BF16)
+        for step in range(0, CHUNK, 2):
+            edges = []
+            for at in (step, step + 1):
+                frame = frames_ref[recv_start + start + at].astype(F32).astype(BF16)
+                half = left_rows[at : at + 1] + jnp.where(frame_col == frame, right_same, right)
+                turn = jnp.tanh(half)
+                gain = half * turn
+                edge = half + gain
+                slope_ref[0, start + at] = (one + turn) * (one + (half - gain))
+                edge_s[start + at] = edge
+                edges.append(edge)
+            wide = wide_ref[0, pl.ds(start + step, 2)].reshape(4 * heads, edge_width)
+            both = dot(wide, jnp.concatenate(edges, axis=0), 1, 1)
+            for at in (0, 1):
+                part = both[2 * heads * at : 2 * heads * (at + 1), block * at : block * (at + 1)]
+                here = start + step + at
+                logit_ref[0, here] = logit_ref[0, here] + part[:heads]
+                dprob_ref[0, here] = dprob_ref[0, here] + part[heads:]
         return carry
 
     lax.fori_loop(0, block // CHUNK, edge_step, 0)
@@ -150,21 +156,23 @@
         pair = jnp.concatenate(
             [probs.reshape(CHUNK, heads, block), weighted.reshape(CHUNK, heads, block)], axis=1
         ).astype(BF16)
-        for step in range(CHUNK):
-            at = start + step
-            sums_ref[0, at] = dot(pair[step], edge_s[at]).astype(BF16)
+        for step in range(0, CHUNK, 2):
+            edges = jnp.concatenate([edge_s[start + step], edge_s[start + step + 1]], axis=1)
+            both = dot(pair[step : step + 2].reshape(4 * heads, block), edges).astype(BF16)
+            sums_ref[0, start + step] = both[: 2 * heads, :edge_width]
+            sums_ref[0, start + step + 1] = both[2 * heads :, edge_width:]
         return carry
 
     lax.fori_loop(0, block // CHUNK, soft_step, 0)
-    stats_ref[0, 3] = jnp.full(stats_ref.shape[2:], local_ref[slot].astype(F32), F32)
+    stats_ref[0, 3] = jnp.full(stats_ref.shape[2:], pairs_ref[0, slot].astype(F32), F32)
     ctx = sums_ref[0].astype(F32)[:, :heads].reshape(block * heads, edge_width).astype(BF16)
     att_ref[0] = gather_heads(dot(probs_s[...], values) + dot(ctx, wev_ref[...]), heads)
 
 
 def backward_kernel(
     scale,
-    local_ref,
-    table_ref,
+    own_blocks,
+    pairs_ref,
     mask_ref,
     nodes_ref,
     dout_ref,
@@ -193,6 +201,7 @@
     ctx_s,
     left_s,
     right_s,
+    diagonal_s,
 ):
     slot = pl.program_id(0)
     heads = logit_ref.shape[2]
@@ -207,12 +216,12 @@
         grad_ev_ref[...] = jnp.zeros_like(grad_ev_ref)
         grad_bias_ref[...] = jnp.zeros_like(grad_bias_ref)
         node_ref[...] = jnp.zeros_like(node_ref)
+        diagonal_s[...] = jnp.zeros_like(diagonal_s)
         leaving_ref[...] = jnp.zeros_like(leaving_ref)
         att_ref[...] = jnp.zeros_like(att_ref)
 
-    local = local_ref[slot]
-    place = table_ref[slot]
-    own_blocks = node_ref.shape[0]
+    local = pairs_ref[0, slot] % own_blocks
+    place = table_place(own_blocks, slot, pairs_ref)
     right_s[...] = jnp.zeros_like(right_s)
 
     def step_group(group, carry):
@@ -242,12 +251,21 @@
         ).astype(BF16)
         right_sum = right_s[...]
         lefts = []
-        for step in range(CHUNK):
-            at = start + step
-            d_edge = dot(pair[step], wide_ref[0, at], 0, 0)
-            d_pre = d_edge * slope_ref[0, at].astype(F32)
-            right_sum = right_sum + d_pre
-            lefts.append(jnp.sum(d_pre, axis=0, keepdims=True))
+        for half in range(CHUNK // GROUP):
+            first = half * GROUP
+            for step in range(GROUP):
+                diagonal_s[
+                    half,
+                    2 * heads * step : 2 * heads * (step + 1),
+                    edge_width * step : edge_width * (step + 1),
+                ] = wide_ref[0, start + first + step]
+            pairs = pair[first : first + GROUP].reshape(GROUP * 2 * heads, block)
+            d_edges = dot(pairs, diagonal_s[half], 0, 0)
+            for step in range(GROUP):
+                slope = slope_ref[0, start + first + step].astype(F32)
+                d_pre = d_edges[:, edge_width * step : edge_width * (step + 1)] * slope
+                right_sum = right_sum + d_pre
+                lefts.append(jnp.sum(d_pre, axis=0, keepdims=True))
         right_s[...] = right_sum
         left_s[pl.ds(start, CHUNK), :] = jnp.concatenate(lefts, axis=0)
         return carry
@@ -320,7 +338,7 @@
 
 
 def fetch_kernel(
-    n_recv, pairs_ref, nodes_ref, got_ref, asked_ref, want_s, ask_s, reply_s, got_s, ask_sems, reply_sems
+    n_recv, pairs_ref, nodes_ref, table_ref, asked_ref, want_s, ask_s, reply_s, got_s, ask_sems, reply_sems
 ):
     me, peers = peers_of("recv", n_recv)
     blocks = nodes_ref.shape[0]
@@ -345,12 +363,13 @@
         reply_s[offset] = reply.astype(BF16)
         replies += post("recv", [peer], reply_sems, lambda target: reply_s.at[offset], got_s.at[me])
     asked_ref[...] = jnp.zeros_like(asked_ref)
-    got_ref[...] = jnp.zeros_like(got_ref)
+    table_ref[:blocks] = nodes_ref[...]
+    table_ref[blocks + me] = jnp.zeros_like(nodes_ref[0])
     for _, target, _ in peers:
         asked_ref[target] = ask_s[target]
     for copy, (_, _, source) in zip(replies, peers):
         copy.wait_recv()
-        got_ref[source] = got_s[source]
+        table_ref[blocks + source] = got_s[source]
     for copy in asks + replies:
         copy.wait_send()
 
@@ -427,16 +446,18 @@
     rows = blocks * block
     share = rows // n_send
     ev_share = ev_ref.shape[0] // n_send
-    bias_rows = bias_ref.shape[0]
+    heads, edge_width = bias_ref.shape
+    sums = att_ref[...].reshape(rows, width)
     meet([("recv", row_peers), ("send", col_peers)])
     backs = post("recv", row_peers, back_sems, lambda target: leaving_ref.at[target], back_s.at[row])
     for part in range(n_send):
-        out_a[part, :share] = att_ref[part * share : (part + 1) * share].astype(BF16)
+        out_a[part, :share] = sums[part * share : (part + 1) * share].astype(BF16)
         out_a[part, share : share + ev_share] = ev_ref[
             part * ev_share : (part + 1) * ev_share
         ].astype(BF16)
-        bias = bias_ref[...] if part == 0 else jnp.zeros_like(bias_ref)
-        out_a[part, share + ev_share :] = bias.astype(BF16)
+        out_a[part, share + ev_share :] = jnp.zeros((BIAS_ROWS, width), BF16)
+    bias = jnp.concatenate([bias_ref[...], jnp.zeros_like(bias_ref)], axis=0).astype(BF16)
+    out_a[0, share + ev_share :, :edge_width] = bias
     sent_a = post("send", col_peers, a_sems, lambda target: out_a.at[target], in_a.at[col])
     acc_s[...] = node_ref[...].reshape(rows, width)
     total = out_a[col].astype(F32)
@@ -480,7 +501,7 @@
         copy.wait_recv()
     for part in range(n_send):
         ev_out_ref[part * ev_share : (part + 1) * ev_share, :] = small_all[part, :ev_share].astype(F32)
-    bias_out_ref[...] = small_all[0, ev_share : ev_share + bias_rows].astype(F32)
+    bias_out_ref[...] = small_all[0, ev_share:, :edge_width].astype(F32)[:heads]
     for copy in fins:
         copy.wait_recv()
     for part in range(n_send):
@@ -488,6 +509,13 @@
         grad_ref[span, :] = dout_ref[span, :].astype(F32) + fin_s[part].astype(F32)
     for copy in backs + sent_a + smalls + mixes + sent_n + small_alls + fins:
         copy.wait_send()
+
+
+def table_place(own_blocks, slot, pairs):
+    owner = pairs[1, slot] // own_blocks
+    return jnp.where(
+        owner == pairs[0, slot] // own_blocks, pairs[1, slot] % own_blocks, own_blocks + owner
+    )
 
 
 def whole_spec(array):
@@ -522,25 +550,18 @@
     heads, edge_width = w_bias.shape
     att_width = w_query.shape[1]
     scale = (att_width // heads) ** (-0.5)
-    my_recv = lax.axis_index("recv")
     n_recv = lax.axis_size("recv")
     n_send = lax.axis_size("send")
-    base_block = my_recv * nb_local
-
-    send_blocks = pairs[1]
-    local_blocks = pairs[0] - base_block
-    owners = send_blocks // nb_local
-    remote = owners != my_recv
-    owner_ids = jnp.arange(n_recv, dtype=jnp.int32)
+
     node_blocks = nodes.reshape(nb_local, block, width)
     in_vmem = pl.BlockSpec(memory_space=pltpu.VMEM)
     asks_shape = (n_recv, 8, 128)
-    got, asked = pl.pallas_call(
+    table, asked = pl.pallas_call(
         functools.partial(fetch_kernel, n_recv),
         in_specs=[pl.BlockSpec(memory_space=pltpu.SMEM), in_vmem],
         out_specs=[in_vmem] * 2,
         out_shape=[
-            jax.ShapeDtypeStruct((n_recv, block, width), BF16),
+            jax.ShapeDtypeStruct((nb_local + n_recv, block, width), BF16),
             jax.ShapeDtypeStruct(asks_shape, F32),
         ],
         scratch_shapes=[
@@ -556,14 +577,14 @@
         ),
         name="fetch",
     )(pairs, node_blocks)
-    table = jnp.concatenate([node_blocks, got], axis=0)
-    table_at = jnp.where(remote, nb_local + owners, send_blocks - base_block)
 
     frame_rows = frames.reshape(-1, 1, block)
     mask_rows = masks.reshape(slots, 1, block)
     edge_row = frame_edge.reshape(1, edge_width)
-    recv_spec = pl.BlockSpec((block, width), lambda slot, local, *_: (local[slot], 0))
-    sender_spec = pl.BlockSpec((1, block, width), lambda slot, local, at, *_: (at[slot], 0, 0))
+    recv_spec = pl.BlockSpec((block, width), lambda slot, pairs, *_: (pairs[0, slot] % nb_local, 0))
+    sender_spec = pl.BlockSpec(
+        (1, block, width), lambda slot, pairs, *_: (table_place(nb_local, slot, pairs), 0, 0)
+    )
     logit_shape = (slots, block, heads, block)
     sums_shape = (slots, block, 2 * heads, edge_width)
     slope_shape = (slots, block, block, edge_width)
@@ -571,12 +592,12 @@
     stats_shape = (slots, 4, block * heads // 128, 128)
     weights = (w_query, w_key, w_value, w_left, w_right, edge_row, w_bias, w_edge_value, w_out)
     forward = pl.pallas_call(
-        functools.partial(forward_kernel, scale),
+        functools.partial(forward_kernel, scale, nb_local),
         grid_spec=pltpu.PrefetchScalarGridSpec(
-            num_scalar_prefetch=5,
+            num_scalar_prefetch=2,
             grid=(slots,),
             in_specs=[
-                pl.BlockSpec((1, 1, block), lambda slot, local, at, recv, send, *_: (send[slot], 0, 0)),
+                pl.BlockSpec((1, 1, block), lambda slot, pairs, *_: (pairs[1, slot], 0, 0)),
                 slot_spec(mask_rows.shape),
                 recv_spec,
                 recv_spec,
@@ -608,7 +629,7 @@
         name="forward",
     )
     logits, dprobs, slopes, sums, wides, att_parts, stats = forward(
-        local_blocks, table_at, pairs[0], send_blocks, frames,
+        pairs, frames,
         frame_rows, mask_rows, nodes, d_out, table, *weights,
     )
 
@@ -633,9 +654,9 @@
     away_shape = (n_recv, block, width)
     att_sum_shape = (nb_local, block, att_width)
     backward = pl.pallas_call(
-        functools.partial(backward_kernel, scale),
+        functools.partial(backward_kernel, scale, nb_local),
         grid_spec=pltpu.PrefetchScalarGridSpec(
-            num_scalar_prefetch=2,
+            num_scalar_prefetch=1,
             grid=(slots,),
             in_specs=[slot_spec(mask_rows.shape), recv_spec, recv_spec, sender_spec]
             + [whole_spec(weight) for weight in weights]
@@ -648,7 +669,7 @@
             ],
             out_specs=[
                 whole_spec(node_blocks),
-                whole_spec(got),
+                whole_spec(jax.ShapeDtypeStruct(away_shape, BF16)),
                 whole_spec(jax.ShapeDtypeStruct(att_sum_shape, F32)),
                 whole_spec(w_edge_value),
                 whole_spec(w_bias),
@@ -659,6 +680,7 @@
                 pltpu.VMEM((block * heads, edge_width), BF16),
                 pltpu.VMEM((block, edge_width), F32),
                 pltpu.VMEM((block, edge_width), F32),
+                pltpu.VMEM((CHUNK // GROUP, GROUP * 2 * heads, GROUP * edge_width), BF16),
             ],
         ),
         out_shape=[
@@ -672,23 +694,21 @@
         name="backward",
     )
     node_sum, leaving, att, grad_ev, grad_bias = backward(
-        local_blocks, table_at, mask_rows, nodes, d_out, table, *weights,
+        pairs, mask_rows, nodes, d_out, table, *weights,
         logits, dprobs, slopes, sums, wides, att_parts, stats, joined,
     )
 
     share = rows // n_send
     ev_share = edge_width // n_send
-    bias_rows = heads * edge_width // att_width
-    bias_flat = jnp.pad(grad_bias.reshape(bias_rows, att_width), ((0, 16 - bias_rows), (0, 0)))
-    tail_rows = ev_share + 16
-    mixed, grad_nodes, bias_flat, grad_ev = pl.pallas_call(
+    tail_rows = ev_share + BIAS_ROWS
+    return pl.pallas_call(
         functools.partial(tail_kernel, n_recv, n_send),
         in_specs=[in_vmem] * 9,
         out_specs=[in_vmem] * 4,
         out_shape=[
             jax.ShapeDtypeStruct((rows, width), BF16),
             jax.ShapeDtypeStruct((rows, width), F32),
-            jax.ShapeDtypeStruct((16, att_width), F32),
+            jax.ShapeDtypeStruct((heads, edge_width), F32),
             jax.ShapeDtypeStruct((edge_width, att_width), F32),
         ],
         scratch_shapes=[
@@ -711,12 +731,10 @@
             pltpu.SemaphoreType.DMA((2, n_send)),
         ],
         compiler_params=pltpu.CompilerParams(
-            collective_id=3, has_side_effects=True, vmem_limit_bytes=VMEM_LIMIT
+            collective_id=3, has_side_effects=True, vmem_limit_bytes=TAIL_LIMIT
         ),
         name="tail",
-    )(att.reshape(rows, att_width), node_sum, leaving, asked, grad_ev, bias_flat, nodes, d_out, w_out)
-    grad_bias = bias_flat[:bias_rows].reshape(heads, edge_width)
-    return (mixed, grad_nodes, grad_bias, grad_ev)
+    )(att, node_sum, leaving, asked, grad_ev, grad_bias, nodes, d_out, w_out)
 
 
 def solution(mesh):

time: 133 us -> 122 us (0.917)
  Pallas kernels: 119 us -> 113 us
  other arithmetic: 3.47 us -> 0 us
  local copies, waits for them, and re-layouts: 8.98 us -> 7.47 us
    pallas_call x2, Pallas kernels: 60.9 us -> 57.2 us  [the longest x1 32.3 us: body(): forward(pairs, frames, frame_rows, mask_rows, nodes, d_out, table, *weights)]
    unnamed x3 -> x22, local copies, waits for them, and re-layouts: 5.1 us -> 7.47 us
    pallas_call x1, Pallas kernels: 29.5 us -> 27.2 us  [body(): pl.pallas_call(functools.partial(tail_kernel, n_recv, n_send), in_specs=[...]
    concatenate x1 -> x0, other arithmetic: 2.11 us -> none  [body(): table = jnp.concatenate([node_blocks, got], axis=0)]
    select_n x1 -> x0, other arithmetic: 1.36 us -> none  [body(): table_at = jnp.where(remote, nb_local + owners, send_blocks - base_block)]
where the time goes in v4:
time: 122 us; the launch traced here: 121 us
  Pallas kernels  113 us (93%)
  local copies, waits for them, and re-layouts  7.47 us (6%)
    pallas_call x1, Pallas kernels, body(): forward(pairs, frames, frame_rows, mask_rows, nodes, d_out, table, *weights)  32.3 us
    pallas_call x1, Pallas kernels, body(): pl.pallas_call(functools.partial(tail_kernel, n_recv, n_send), in_specs=[...  27.2 us
    pallas_call x1, Pallas kernels, body(): backward(pairs, mask_rows, nodes, d_out, table, *weights, logits, dprobs,...  24.9 us
    pallas_call x1, Pallas kernels, body(): pl.pallas_call(functools.partial(fetch_kernel, n_recv), in_specs=[pl.Bloc...  21.7 us
    unnamed x22, local copies, waits for them, and re-layouts  7.47 us
    pallas_call x1, Pallas kernels, body(): pl.pallas_call(functools.partial(join_kernel, n_send), in_specs=[in_vmem]...  6.56 us

profile of v4, /device:TPU:0, one launch (start us, length us, event | category | flops | bytes accessed | tf_op | source)
XLA Modules:
  0.0 120.9 jit_solution(4620765642354048664)
XLA Ops:
  0.6 21.7 %fetch.1 = (bf16[12,128,256]{2,1,0:T(8,128)(2,1)}, f32[8,8,128]{2,1,0:T(8,128)}) custom-call(s32[2,4]{1,0:T(2,128)} %pairs_ref.5, bf16[4,128,256]{2,1,0:T(8,128)(2,1)} %bitcast.4), custom_call_target="tpu_custom_call" | custom-call | tf_op jit(solution)/shard_map/fetch/pallas_call | solution.py:559
  22.4 32.3 %forward.1 = (f32[4,128,8,128]{3,2,1,0:T(8,128)}, f32[4,128,8,128]{3,2,1,0:T(8,128)}, bf16[4,128,128,128]{3,2,1,0:T(8,128)(2,1)}, bf16[4,128,16,128]{3,2,1,0:T(8...) custom-call(s32[2,4]{1,0:T(2,128)} %pairs_ref.5, ...), custom_call_target="tpu_custom_call" | custom-call | tf_op jit(solution)/shard_map/forward/pallas_call | solution.py:631
  54.7 6.6 %join.1.joined_ref = f32[4,2,8,128]{3,2,1,0:T(8,128)} custom-call(f32[4,4,8,128]{3,2,1,0:T(8,128)} %get-tuple-element.25.stats_ref), custom_call_target="tpu_custom_call" | custom-call | tf_op jit(solution)/shard_map/join/pallas_call | solution.py:637
  61.3 0.0 copy-start
  61.3 0.0 copy-start.1
  61.3 0.0 copy-start.2
  61.3 0.0 copy-start.7
  61.3 24.9 %backward.1 = (f32[4,128,256]{2,1,0:T(8,128)}, bf16[8,128,256]{2,1,0:T(8,128)(2,1)}, f32[4,128,256]{2,1,0:T(8,128)}, f32[128,256]{1,0:T(8,128)}, f32[8,128]{1,0:T(8,128)}) custom-call(s32[2,4]{1,0:T(2,128)} %pairs_ref.5, s32[4,1,128]{2,1,0:T(1,128)} %bitcast.7, bf16[512,256]{1,0:T(8,128)(2,1)} %nodes_ref.5, bf16[512,256]{1,0:T(8,128)(2,1)} %dout_ref.5, ...), custom_call_target="tpu_custom_call" | custom-call | tf_op jit(solution)/shard_map/backward/pallas_call | solution.py:696
  86.2 0.0 copy-done
  86.2 0.0 copy-done.1
  86.2 0.0 copy-done.2
  86.2 0.0 copy-done.7
  86.2 0.0 copy-start.3
  86.3 1.0 copy-done.3
  87.3 0.0 copy-start.4
  87.3 1.0 copy-done.4
  88.3 0.0 copy-start.5
  88.3 1.0 copy-done.5
  89.4 0.0 copy-start.6
  89.4 0.9 copy-done.6
  90.3 0.0 copy-start.8
  90.3 0.7 copy-done.8
  91.0 27.2 %tail.1 = (bf16[512,256]{1,0:T(8,128)(2,1)S(1)}, f32[512,256]{1,0:T(8,128)S(1)}, f32[8,128]{1,0:T(8,128)S(1)}, f32[128,256]{1,0:T(8,128)S(1)}) custom-call(f32[4,128,256]{2,1,0:T(8,128)S(1)} %copy-done.5, f32[4,128,256]{2,1,0:T(8,128)S(1)} %copy-done.3, bf16[8,128,256]{2,1,0:T(8,128)(2,1)S(1)} %copy-done.4, f32[8,8,128]{2,1,0:T(8,128)S(1)} %copy-done.7, ...), custom_call_target="tpu_custom_call" | custom-call | tf_op jit(solution)/shard_map/tail/pallas_call | solution.py:704
  118.1 0.7 copy.22
  118.8 0.8 copy.23
  119.6 0.6 copy.24
  120.2 0.7 copy.25
Async XLA Ops:
  61.3 24.9 %copy-start = (bf16[512,256]{1,0:T(8,128)(2,1)S(1)}, bf16[512,256]{1,0:T(8,128)(2,1)}, u32[]{:S(2)}) copy-start(bf16[512,256]{1,0:T(8,128)(2,1)} %nodes_ref.5) | copy-start | bytes 786436
  61.3 24.9 %copy-start.1 = (bf16[512,256]{1,0:T(8,128)(2,1)S(1)}, bf16[512,256]{1,0:T(8,128)(2,1)}, u32[]{:S(2)}) copy-start(bf16[512,256]{1,0:T(8,128)(2,1)} %dout_ref.5) | copy-start | bytes 786436
  61.3 24.9 %copy-start.2 = (bf16[256,256]{1,0:T(8,128)(2,1)S(1)}, bf16[256,256]{1,0:T(8,128)(2,1)}, u32[]{:S(2)}) copy-start(bf16[256,256]{1,0:T(8,128)(2,1)} %wo_ref.5) | copy-start | bytes 393220
  61.3 24.9 %copy-start.7 = (f32[8,8,128]{2,1,0:T(8,128)S(1)}, f32[8,8,128]{2,1,0:T(8,128)}, u32[]{:S(2)}) copy-start(f32[8,8,128]{2,1,0:T(8,128)} %get-tuple-element.29.asked_ref) | copy-start | bytes 98308
  86.2 1.0 copy-start.3
  87.3 1.0 copy-start.4
  88.3 1.0 copy-start.5
  89.4 0.9 copy-start.6
  90.3 0.7 copy-start.8

commit v5 on v4

--- a/solution.py
+++ b/solution.py
@@ -9,10 +9,11 @@
 
 NEG_LARGE = -1e30
 CHUNK = 16
+WIDE_CHUNK = 32
 GROUP = 8
 BIAS_ROWS = 16
 VMEM_LIMIT = 60 * 2**20
-TAIL_LIMIT = 32 * 2**20
+TAIL_LIMIT = 60 * 2**20
 F32 = jnp.float32
 BF16 = jnp.bfloat16
 
@@ -45,17 +46,25 @@
     ) == lax.broadcasted_iota(jnp.int32, (heads, width), 0)
 
 
+def owner_matrix(count, heads, rows_first):
+    shape = (count * heads, count) if rows_first else (count, count * heads)
+    wide = lax.broadcasted_iota(jnp.int32, shape, 0 if rows_first else 1) // heads
+    narrow = lax.broadcasted_iota(jnp.int32, shape, 1 if rows_first else 0)
+    return jnp.where(wide == narrow, 1.0, 0.0).astype(BF16)
+
+
 def spread(rows, heads):
     count, width = rows.shape
     mask = head_mask(heads, width)
-    wide = jnp.where(mask[None], rows.astype(F32)[:, None, :], 0.0)
-    return wide.reshape(count * heads, width).astype(BF16)
+    wide = dot(owner_matrix(count, heads, True), rows).reshape(count, heads, width)
+    return jnp.where(mask[None], wide, 0.0).reshape(count * heads, width).astype(BF16)
 
 
 def gather_heads(wide, heads):
     count, width = wide.shape
     mask = head_mask(heads, width)
-    return jnp.sum(jnp.where(mask[None], wide.reshape(count // heads, heads, width), 0.0), axis=1)
+    kept = jnp.where(mask[None], wide.reshape(count // heads, heads, width), 0.0)
+    return dot(owner_matrix(count // heads, heads, False), kept.reshape(count, width).astype(BF16))
 
 
 def forward_kernel(
@@ -87,6 +96,8 @@
     left_s,
     edge_s,
     probs_s,
+    scores_s,
+    dvalues_s,
 ):
     slot = pl.program_id(0)
     heads, edge_width = wb_ref.shape
@@ -105,8 +116,8 @@
         to_column(frame_row_ref[0].astype(F32)), (block, edge_width)
     ).astype(BF16)
     datt_wide = spread(datt, heads)
-    logit_ref[0] = (dot(spread(query, heads), keys, 1, 1) * scale).reshape(block, heads, block)
-    dprob_ref[0] = dot(datt_wide, values, 1, 1).reshape(block, heads, block)
+    scores_s[...] = (dot(spread(query, heads), keys, 1, 1) * scale).reshape(block, heads, block)
+    dvalues_s[...] = dot(datt_wide, values, 1, 1).reshape(block, heads, block)
     dctx = dot(datt_wide, wev_ref[...], 1, 1).reshape(block, heads, edge_width)
     bias = jnp.broadcast_to(wb_ref[...].astype(F32)[None], dctx.shape)
     wide_ref[0] = jnp.concatenate([bias, dctx], axis=1).astype(BF16)
@@ -115,9 +126,9 @@
     one = jnp.ones((), BF16)
 
     def edge_step(group, carry):
-        start = group * CHUNK
-        left_rows = left_s[pl.ds(start, CHUNK), :].astype(BF16)
-        for step in range(0, CHUNK, 2):
+        start = group * WIDE_CHUNK
+        left_rows = left_s[pl.ds(start, WIDE_CHUNK), :].astype(BF16)
+        for step in range(0, WIDE_CHUNK, 2):
             edges = []
             for at in (step, step + 1):
                 frame = frames_ref[recv_start + start + at].astype(F32).astype(BF16)
@@ -133,37 +144,39 @@
             for at in (0, 1):
                 part = both[2 * heads * at : 2 * heads * (at + 1), block * at : block * (at + 1)]
                 here = start + step + at
-                logit_ref[0, here] = logit_ref[0, here] + part[:heads]
-                dprob_ref[0, here] = dprob_ref[0, here] + part[heads:]
+                logit_ref[0, here] = scores_s[here] + part[:heads]
+                dprob_ref[0, here] = dvalues_s[here] + part[heads:]
         return carry
 
-    lax.fori_loop(0, block // CHUNK, edge_step, 0)
+    lax.fori_loop(0, block // WIDE_CHUNK, edge_step, 0)
     valid = mask_ref[0] > 0
 
-    def soft_step(group, carry):
-        start = group * CHUNK
-        rows = pl.ds(start * heads, CHUNK * heads)
-        logits = logit_ref[0, pl.ds(start, CHUNK)].reshape(CHUNK * heads, block)
-        dprob = dprob_ref[0, pl.ds(start, CHUNK)].reshape(CHUNK * heads, block)
-        logits = jnp.where(valid, logits, NEG_LARGE)
-        top = jnp.max(logits, axis=1, keepdims=True)
-        probs = jnp.where(valid, jnp.exp(logits - top), 0.0)
-        weighted = probs * dprob
-        stats_ref[0, 0, pl.ds(group, 1), :] = to_row(top)
-        stats_ref[0, 1, pl.ds(group, 1), :] = to_row(jnp.sum(probs, axis=1, keepdims=True))
-        stats_ref[0, 2, pl.ds(group, 1), :] = to_row(jnp.sum(weighted, axis=1, keepdims=True))
-        probs_s[rows, :] = probs.astype(BF16)
-        pair = jnp.concatenate(
-            [probs.reshape(CHUNK, heads, block), weighted.reshape(CHUNK, heads, block)], axis=1
-        ).astype(BF16)
-        for step in range(0, CHUNK, 2):
-            edges = jnp.concatenate([edge_s[start + step], edge_s[start + step + 1]], axis=1)
-            both = dot(pair[step : step + 2].reshape(4 * heads, block), edges).astype(BF16)
-            sums_ref[0, start + step] = both[: 2 * heads, :edge_width]
-            sums_ref[0, start + step + 1] = both[2 * heads :, edge_width:]
+    def soft_step(step_at, carry):
+        for sub in range(WIDE_CHUNK // CHUNK):
+            group = step_at * (WIDE_CHUNK // CHUNK) + sub
+            start = group * CHUNK
+            rows = pl.ds(start * heads, CHUNK * heads)
+            logits = logit_ref[0, pl.ds(start, CHUNK)].reshape(CHUNK * heads, block)
+            dprob = dprob_ref[0, pl.ds(start, CHUNK)].reshape(CHUNK * heads, block)
+            logits = jnp.where(valid, logits, NEG_LARGE)
+            top = jnp.max(logits, axis=1, keepdims=True)
+            probs = jnp.where(valid, jnp.exp(logits - top), 0.0)
+            weighted = probs * dprob
+            stats_ref[0, 0, pl.ds(group, 1), :] = to_row(top)
+            stats_ref[0, 1, pl.ds(group, 1), :] = to_row(jnp.sum(probs, axis=1, keepdims=True))
+            stats_ref[0, 2, pl.ds(group, 1), :] = to_row(jnp.sum(weighted, axis=1, keepdims=True))
+            probs_s[rows, :] = probs.astype(BF16)
+            pair = jnp.concatenate(
+                [probs.reshape(CHUNK, heads, block), weighted.reshape(CHUNK, heads, block)], axis=1
+            ).astype(BF16)
+            for step in range(0, CHUNK, 2):
+                edges = jnp.concatenate([edge_s[start + step], edge_s[start + step + 1]], axis=1)
+                both = dot(pair[step : step + 2].reshape(4 * heads, block), edges).astype(BF16)
+                sums_ref[0, start + step] = both[: 2 * heads, :edge_width]
+                sums_ref[0, start + step + 1] = both[2 * heads :, edge_width:]
         return carry
 
-    lax.fori_loop(0, block // CHUNK, soft_step, 0)
+    lax.fori_loop(0, block // WIDE_CHUNK, soft_step, 0)
     stats_ref[0, 3] = jnp.full(stats_ref.shape[2:], pairs_ref[0, slot].astype(F32), F32)
     ctx = sums_ref[0].astype(F32)[:, :heads].reshape(block * heads, edge_width).astype(BF16)
     att_ref[0] = gather_heads(dot(probs_s[...], values) + dot(ctx, wev_ref[...]), heads)
@@ -224,53 +237,55 @@
     place = table_place(own_blocks, slot, pairs_ref)
     right_s[...] = jnp.zeros_like(right_s)
 
-    def step_group(group, carry):
-        start = group * CHUNK
-        rows = pl.ds(start * heads, CHUNK * heads)
-        lse = joined_ref[0, 0, pl.ds(group, 1), :]
-        lse_col = to_column(lse)
-        delta_col = to_column(joined_ref[0, 1, pl.ds(group, 1), :])
-        factor_col = to_column(jnp.exp(stats_ref[0, 0, pl.ds(group, 1), :] - lse))
-        logits = logit_ref[0, pl.ds(start, CHUNK)].reshape(CHUNK * heads, block)
-        dprob = dprob_ref[0, pl.ds(start, CHUNK)].reshape(CHUNK * heads, block)
-        probs = jnp.where(valid, jnp.exp(logits - lse_col), 0.0)
-        dlogit = probs * (dprob - delta_col)
-        probs_s[rows, :] = probs.astype(BF16)
-        dlogit_s[rows, :] = dlogit.astype(BF16)
-        sums = sums_ref[0, pl.ds(start, CHUNK)].astype(F32)
-        ctx = sums[:, :heads].reshape(CHUNK * heads, edge_width) * factor_col
-        ctx_s[rows, :] = ctx.astype(BF16)
-        moved = sums[:, heads:].reshape(CHUNK * heads, edge_width) * factor_col - ctx * delta_col
-        grad_bias_ref[...] += jnp.sum(moved.reshape(CHUNK, heads, edge_width), axis=0)
-        factor = jnp.sum(
-            jnp.where(mask[None], factor_col.reshape(CHUNK, heads, 1), 0.0), axis=1
-        )
-        att_ref[local, pl.ds(start, CHUNK), :] += att_in_ref[0, pl.ds(start, CHUNK), :] * factor
-        pair = jnp.concatenate(
-            [dlogit.reshape(CHUNK, heads, block), probs.reshape(CHUNK, heads, block)], axis=1
-        ).astype(BF16)
-        right_sum = right_s[...]
-        lefts = []
-        for half in range(CHUNK // GROUP):
-            first = half * GROUP
-            for step in range(GROUP):
-                diagonal_s[
-                    half,
-                    2 * heads * step : 2 * heads * (step + 1),
-                    edge_width * step : edge_width * (step + 1),
-                ] = wide_ref[0, start + first + step]
-            pairs = pair[first : first + GROUP].reshape(GROUP * 2 * heads, block)
-            d_edges = dot(pairs, diagonal_s[half], 0, 0)
-            for step in range(GROUP):
-                slope = slope_ref[0, start + first + step].astype(F32)
-                d_pre = d_edges[:, edge_width * step : edge_width * (step + 1)] * slope
-                right_sum = right_sum + d_pre
-                lefts.append(jnp.sum(d_pre, axis=0, keepdims=True))
-        right_s[...] = right_sum
-        left_s[pl.ds(start, CHUNK), :] = jnp.concatenate(lefts, axis=0)
+    def step_group(step_at, carry):
+        for sub in range(WIDE_CHUNK // CHUNK):
+            group = step_at * (WIDE_CHUNK // CHUNK) + sub
+            start = group * CHUNK
+            rows = pl.ds(start * heads, CHUNK * heads)
+            lse = joined_ref[0, 0, pl.ds(group, 1), :]
+            lse_col = to_column(lse)
+            delta_col = to_column(joined_ref[0, 1, pl.ds(group, 1), :])
+            factor_col = to_column(jnp.exp(stats_ref[0, 0, pl.ds(group, 1), :] - lse))
+            logits = logit_ref[0, pl.ds(start, CHUNK)].reshape(CHUNK * heads, block)
+            dprob = dprob_ref[0, pl.ds(start, CHUNK)].reshape(CHUNK * heads, block)
+            probs = jnp.where(valid, jnp.exp(logits - lse_col), 0.0)
+            dlogit = probs * (dprob - delta_col)
+            probs_s[rows, :] = probs.astype(BF16)
+            dlogit_s[rows, :] = dlogit.astype(BF16)
+            sums = sums_ref[0, pl.ds(start, CHUNK)].astype(F32)
+            ctx = sums[:, :heads].reshape(CHUNK * heads, edge_width) * factor_col
+            ctx_s[rows, :] = ctx.astype(BF16)
+            moved = sums[:, heads:].reshape(CHUNK * heads, edge_width) * factor_col - ctx * delta_col
+            grad_bias_ref[...] += jnp.sum(moved.reshape(CHUNK, heads, edge_width), axis=0)
+            factor = jnp.sum(
+                jnp.where(mask[None], factor_col.reshape(CHUNK, heads, 1), 0.0), axis=1
+            )
+            att_ref[local, pl.ds(start, CHUNK), :] += att_in_ref[0, pl.ds(start, CHUNK), :] * factor
+            pair = jnp.concatenate(
+                [dlogit.reshape(CHUNK, heads, block), probs.reshape(CHUNK, heads, block)], axis=1
+            ).astype(BF16)
+            right_sum = right_s[...]
+            lefts = []
+            for half in range(CHUNK // GROUP):
+                first = half * GROUP
+                for step in range(GROUP):
+                    diagonal_s[
+                        sub * (CHUNK // GROUP) + half,
+                        2 * heads * step : 2 * heads * (step + 1),
+                        edge_width * step : edge_width * (step + 1),
+                    ] = wide_ref[0, start + first + step]
+                pairs = pair[first : first + GROUP].reshape(GROUP * 2 * heads, block)
+                d_edges = dot(pairs, diagonal_s[sub * (CHUNK // GROUP) + half], 0, 0)
+                for step in range(GROUP):
+                    slope = slope_ref[0, start + first + step].astype(F32)
+                    d_pre = d_edges[:, edge_width * step : edge_width * (step + 1)] * slope
+                    right_sum = right_sum + d_pre
+                    lefts.append(jnp.sum(d_pre, axis=0, keepdims=True))
+            right_s[...] = right_sum
+            left_s[pl.ds(start, CHUNK), :] = jnp.concatenate(lefts, axis=0)
         return carry
 
-    lax.fori_loop(0, block // CHUNK, step_group, 0)
+    lax.fori_loop(0, block // WIDE_CHUNK, step_group, 0)
     nodes = nodes_ref[...]
     sender = sender_ref[0]
     query_wide = spread(dot(nodes, wq_ref[...]).astype(BF16), heads)
@@ -409,11 +424,11 @@
 def tail_kernel(
     n_recv,
     n_send,
-    att_ref,
-    node_ref,
+    att_hbm,
+    node_hbm,
     leaving_ref,
     asked_ref,
-    ev_ref,
+    ev_hbm,
     bias_ref,
     nodes_ref,
     dout_ref,
@@ -422,6 +437,10 @@
     grad_ref,
     bias_out_ref,
     ev_out_ref,
+    att_ref,
+    node_ref,
+    ev_ref,
+    load_sems,
     back_s,
     out_a,
     in_a,
@@ -447,9 +466,19 @@
     share = rows // n_send
     ev_share = ev_ref.shape[0] // n_send
     heads, edge_width = bias_ref.shape
-    sums = att_ref[...].reshape(rows, width)
+    loads = [
+        pltpu.make_async_copy(source, target, load_sems.at[at])
+        for at, (source, target) in enumerate(
+            ((att_hbm, att_ref), (ev_hbm, ev_ref), (node_hbm, node_ref))
+        )
+    ]
+    for load in loads:
+        load.start()
     meet([("recv", row_peers), ("send", col_peers)])
     backs = post("recv", row_peers, back_sems, lambda target: leaving_ref.at[target], back_s.at[row])
+    loads[0].wait()
+    loads[1].wait()
+    sums = att_ref[...].reshape(rows, width)
     for part in range(n_send):
         out_a[part, :share] = sums[part * share : (part + 1) * share].astype(BF16)
         out_a[part, share : share + ev_share] = ev_ref[
@@ -459,6 +488,7 @@
     bias = jnp.concatenate([bias_ref[...], jnp.zeros_like(bias_ref)], axis=0).astype(BF16)
     out_a[0, share + ev_share :, :edge_width] = bias
     sent_a = post("send", col_peers, a_sems, lambda target: out_a.at[target], in_a.at[col])
+    loads[2].wait()
     acc_s[...] = node_ref[...].reshape(rows, width)
     total = out_a[col].astype(F32)
     for copy, (_, _, source) in zip(sent_a, col_peers):
@@ -555,6 +585,7 @@
 
     node_blocks = nodes.reshape(nb_local, block, width)
     in_vmem = pl.BlockSpec(memory_space=pltpu.VMEM)
+    in_hbm = pl.BlockSpec(memory_space=pltpu.HBM)
     asks_shape = (n_recv, 8, 128)
     table, asked = pl.pallas_call(
         functools.partial(fetch_kernel, n_recv),
@@ -614,6 +645,8 @@
                 pltpu.VMEM((block, edge_width), F32),
                 pltpu.VMEM((block, block, edge_width), BF16),
                 pltpu.VMEM((block * heads, block), BF16),
+                pltpu.VMEM((block, heads, block), F32),
+                pltpu.VMEM((block, heads, block), F32),
             ],
         ),
         out_shape=[
@@ -680,7 +713,7 @@
                 pltpu.VMEM((block * heads, edge_width), BF16),
                 pltpu.VMEM((block, edge_width), F32),
                 pltpu.VMEM((block, edge_width), F32),
-                pltpu.VMEM((CHUNK // GROUP, GROUP * 2 * heads, GROUP * edge_width), BF16),
+                pltpu.VMEM((WIDE_CHUNK // GROUP, GROUP * 2 * heads, GROUP * edge_width), BF16),
             ],
         ),
         out_shape=[
@@ -703,7 +736,7 @@
     tail_rows = ev_share + BIAS_ROWS
     return pl.pallas_call(
         functools.partial(tail_kernel, n_recv, n_send),
-        in_specs=[in_vmem] * 9,
+        in_specs=[in_hbm, in_hbm, in_hbm, in_vmem, in_hbm, in_vmem, in_vmem, in_vmem, in_vmem],
         out_specs=[in_vmem] * 4,
         out_shape=[
             jax.ShapeDtypeStruct((rows, width), BF16),
@@ -712,6 +745,10 @@
             jax.ShapeDtypeStruct((edge_width, att_width), F32),
         ],
         scratch_shapes=[
+            pltpu.VMEM(att_sum_shape, F32),
+            pltpu.VMEM(node_shape, F32),
+            pltpu.VMEM((edge_width, att_width), F32),
+            pltpu.SemaphoreType.DMA((3,)),
             pltpu.VMEM(away_shape, BF16),
             pltpu.VMEM((n_send, share + tail_rows, att_width), BF16),
             pltpu.VMEM((n_send, share + tail_rows, att_width), BF16),

time: 122 us -> 120 us (0.984)
    pallas_call x1, Pallas kernels: 32.3 us -> 29.3 us  [body(): forward(pairs, frames, frame_rows, mask_rows, nodes, d_out, table, *weights)]
    pallas_call x1, Pallas kernels: 27.2 us -> 29.2 us  [body(): pl.pallas_call(functools.partial(tail_kernel, n_recv, n_send), in_specs=[...]
    unnamed x22 -> x4, local copies, waits for them, and re-layouts: 7.47 us -> 6.37 us
where the time goes in v5:
time: 120 us; the launch traced here: 119 us
  Pallas kernels  112 us (93%)
  local copies, waits for them, and re-layouts  6.37 us (5%)
    pallas_call x1, Pallas kernels, body(): forward(pairs, frames, frame_rows, mask_rows, nodes, d_out, table, *weights)  29.3 us
    pallas_call x1, Pallas kernels, body(): pl.pallas_call(functools.partial(tail_kernel, n_recv, n_send), in_specs=[...  29.2 us
    pallas_call x1, Pallas kernels, body(): backward(pairs, mask_rows, nodes, d_out, table, *weights, logits, dprobs,...  24.9 us
    pallas_call x1, Pallas kernels, body(): pl.pallas_call(functools.partial(fetch_kernel, n_recv), in_specs=[pl.Bloc...  21.7 us
    pallas_call x1, Pallas kernels, body(): pl.pallas_call(functools.partial(join_kernel, n_send), in_specs=[in_vmem]...  6.55 us
    unnamed x4, local copies, waits for them, and re-layouts  6.37 us

profile of v5, /device:TPU:0, one launch (start us, length us, event | category | flops | bytes accessed | tf_op | source)
XLA Modules:
  0.0 118.7 jit_solution(13939866276492145887)
XLA Ops:
  0.6 21.7 %fetch.1 = (bf16[12,128,256]{2,1,0:T(8,128)(2,1)}, f32[8,8,128]{2,1,0:T(8,128)}) custom-call(s32[2,4]{1,0:T(2,128)} %pairs_ref.5, bf16[4,128,256]{2,1,0:T(8,128)(2,1)} %bitcast.4), custom_call_target="tpu_custom_call" | custom-call | tf_op jit(solution)/shard_map/fetch/pallas_call | solution.py:590
  22.4 29.3 %forward.1 = (f32[4,128,8,128]{3,2,1,0:T(8,128)}, f32[4,128,8,128]{3,2,1,0:T(8,128)}, bf16[4,128,128,128]{3,2,1,0:T(8,128)(2,1)}, bf16[4,128,16,128]{3,2,1,0:T(8...) custom-call(s32[2,4]{1,0:T(2,128)} %pairs_ref.5, ...), custom_call_target="tpu_custom_call" | custom-call | tf_op jit(solution)/shard_map/forward/pallas_call | solution.py:664
  51.6 6.6 %join.1.joined_ref = f32[4,2,8,128]{3,2,1,0:T(8,128)} custom-call(f32[4,4,8,128]{3,2,1,0:T(8,128)} %get-tuple-element.25.stats_ref), custom_call_target="tpu_custom_call" | custom-call | tf_op jit(solution)/shard_map/join/pallas_call | solution.py:670
  58.2 24.9 %backward.1 = (f32[4,128,256]{2,1,0:T(8,128)}, bf16[8,128,256]{2,1,0:T(8,128)(2,1)}, f32[4,128,256]{2,1,0:T(8,128)}, f32[128,256]{1,0:T(8,128)}, f32[8,128]{1,0:T(8,128)}) custom-call(s32[2,4]{1,0:T(2,128)} %pairs_ref.5, s32[4,1,128]{2,1,0:T(1,128)} %bitcast.7, bf16[512,256]{1,0:T(8,128)(2,1)} %nodes_ref.5, bf16[512,256]{1,0:T(8,128)(2,1)} %dout_ref.5, ...), custom_call_target="tpu_custom_call" | custom-call | tf_op jit(solution)/shard_map/backward/pallas_call | solution.py:729
  83.1 29.2 %tail.1 = (bf16[512,256]{1,0:T(8,128)(2,1)}, f32[512,256]{1,0:T(8,128)}, f32[8,128]{1,0:T(8,128)}, f32[128,256]{1,0:T(8,128)}) custom-call(f32[4,128,256]{2,1,0:T(8,128)} %get-tuple-element.26.att_hbm, f32[4,128,256]{2,1,0:T(8,128)} %get-tuple-element.27.node_hbm, bf16[8,128,256]{2,1,0:T(8,128)(2,1)} %get-tuple-element.28.leaving_ref, ...), custom_call_target="tpu_custom_call" | custom-call | tf_op jit(solution)/shard_map/tail/pallas_call | solution.py:737
  112.3 1.7 %copy.22 = bf16[512,256]{1,0:T(8,128)(2,1)} copy(bf16[512,256]{1,0:T(8,128)(2,1)} %get-tuple-element.36) | data formatting | bytes 524288
  114.0 1.9 %copy.23 = f32[512,256]{1,0:T(8,128)} copy(f32[512,256]{1,0:T(8,128)} %get-tuple-element.37) | data formatting | bytes 1048576
  115.8 1.3 %copy.24 = f32[8,128]{1,0:T(8,128)} copy(f32[8,128]{1,0:T(8,128)} %get-tuple-element.38) | data formatting | bytes 8192
  117.1 1.6 %copy.25 = f32[128,256]{1,0:T(8,128)} copy(f32[128,256]{1,0:T(8,128)} %get-tuple-element.39) | data formatting | bytes 262144

commit v6 on v5

--- a/solution.py
+++ b/solution.py
@@ -13,7 +13,8 @@
 GROUP = 8
 BIAS_ROWS = 16
 VMEM_LIMIT = 60 * 2**20
-TAIL_LIMIT = 60 * 2**20
+TAIL_LIMIT = 40 * 2**20
+BACKWARD_LIMIT = 50 * 2**20
 F32 = jnp.float32
 BF16 = jnp.bfloat16
 
@@ -723,7 +724,7 @@
             jax.ShapeDtypeStruct(w_edge_value.shape, F32),
             jax.ShapeDtypeStruct(w_bias.shape, F32),
         ],
-        compiler_params=pltpu.CompilerParams(vmem_limit_bytes=VMEM_LIMIT),
+        compiler_params=pltpu.CompilerParams(vmem_limit_bytes=BACKWARD_LIMIT),
         name="backward",
     )
     node_sum, leaving, att, grad_ev, grad_bias = backward(

time: 120 us -> 116 us (0.967)
  Pallas kernels: 112 us -> 108 us
    pallas_call x1, Pallas kernels: 29.2 us -> 27.3 us  [body(): pl.pallas_call(functools.partial(tail_kernel, n_recv, n_send), in_specs=[...]
    pallas_call x1, Pallas kernels: 24.9 us -> 23.3 us  [body(): backward(pairs, mask_rows, nodes, d_out, table, *weights, logits, dprobs,...]
    unnamed x4 -> x32, local copies, waits for them, and re-layouts: 6.37 us -> 5.44 us
where the time goes in v6:
time: 116 us; the launch traced here: 115 us
  Pallas kernels  108 us (93%)
  local copies, waits for them, and re-layouts  5.44 us (5%)
    pallas_call x1, Pallas kernels, body(): forward(pairs, frames, frame_rows, mask_rows, nodes, d_out, table, *weights)  29.3 us
    pallas_call x1, Pallas kernels, body(): pl.pallas_call(functools.partial(tail_kernel, n_recv, n_send), in_specs=[...  27.3 us
    pallas_call x1, Pallas kernels, body(): backward(pairs, mask_rows, nodes, d_out, table, *weights, logits, dprobs,...  23.3 us
    pallas_call x1, Pallas kernels, body(): pl.pallas_call(functools.partial(fetch_kernel, n_recv), in_specs=[pl.Bloc...  21.9 us
    pallas_call x1, Pallas kernels, body(): pl.pallas_call(functools.partial(join_kernel, n_send), in_specs=[in_vmem]...  6.54 us
    unnamed x32, local copies, waits for them, and re-layouts  5.44 us

profile of v6, /device:TPU:0, one launch (start us, length us, event | category | flops | bytes accessed | tf_op | source)
XLA Modules:
  0.0 114.5 jit_solution(8937726272684775414)
XLA Ops:
  0.6 0.0 copy-start
  0.6 0.0 copy-start.2
  0.7 0.0 copy-start.1
  0.7 0.0 copy-start.12
  0.7 0.0 copy-start.8
  0.7 0.0 copy-start.7
  0.7 0.0 copy-start.5
  0.7 0.0 copy-start.4
  0.7 0.0 copy-start.3
  0.7 0.0 copy-start.13
  0.8 21.9 %fetch.1 = (bf16[12,128,256]{2,1,0:T(8,128)(2,1)}, f32[8,8,128]{2,1,0:T(8,128)}) custom-call(s32[2,4]{1,0:T(2,128)} %pairs_ref.5, bf16[4,128,256]{2,1,0:T(8,128)(2,1)} %bitcast.4), custom_call_target="tpu_custom_call" | custom-call | tf_op jit(solution)/shard_map/fetch/pallas_call | solution.py:591
  22.6 29.3 %forward.1 = (f32[4,128,8,128]{3,2,1,0:T(8,128)}, f32[4,128,8,128]{3,2,1,0:T(8,128)}, bf16[4,128,128,128]{3,2,1,0:T(8,128)(2,1)}, bf16[4,128,16,128]{3,2,1,0:T(8...) custom-call(s32[2,4]{1,0:T(2,128)} %pairs_ref.5, ...), custom_call_target="tpu_custom_call" | custom-call | tf_op jit(solution)/shard_map/forward/pallas_call | solution.py:665
  51.9 6.5 %join.1.joined_ref = f32[4,2,8,128]{3,2,1,0:T(8,128)} custom-call(f32[4,4,8,128]{3,2,1,0:T(8,128)} %get-tuple-element.25.stats_ref), custom_call_target="tpu_custom_call" | custom-call | tf_op jit(solution)/shard_map/join/pallas_call | solution.py:671
  58.4 0.0 copy-done
  58.4 0.0 copy-done.2
  58.5 0.0 copy-done.1
  58.5 0.0 copy-done.12
  58.5 0.0 copy-done.8
  58.5 0.0 copy-done.7
  58.5 0.0 copy-done.5
  58.5 0.0 copy-done.4
  58.5 0.0 copy-done.3
  58.5 0.0 copy-done.13
  58.5 0.0 copy-start.6
  58.6 1.0 copy-done.6
  59.6 0.0 copy-start.9
  59.6 0.8 copy-done.9
  60.4 0.0 copy-start.10
  60.4 0.8 copy-done.10
  61.2 0.0 copy-start.11
  61.2 23.3 %backward.1 = (f32[4,128,256]{2,1,0:T(8,128)S(1)}, bf16[8,128,256]{2,1,0:T(8,128)(2,1)S(1)}, f32[4,128,256]{2,1,0:T(8,128)S(1)}, f32[128,256]{1,0:T(8,128)S(1)}, f32[8,128]{1,0:T(8,128)S(1)}) custom-call(s32[2,4]{1,0:T(2,128)S(1)} %copy-done.12, s32[4,1,128]{2,1,0:T(1,128)S(1)} %bitcast.6, bf16[512,256]{1,0:T(8,128)(2,1)S(1)} %copy-done, ...), custom_call_target="tpu_custom_call" | custom-call | tf_op jit(solution)/shard_map/backward/pallas_call | solution.py:730
  84.5 0.0 copy-done.11
  84.5 27.3 %tail.1 = (bf16[512,256]{1,0:T(8,128)(2,1)S(1)}, f32[512,256]{1,0:T(8,128)S(1)}, f32[8,128]{1,0:T(8,128)S(1)}, f32[128,256]{1,0:T(8,128)S(1)}) custom-call(f32[4,128,256]{2,1,0:T(8,128)S(1)} %get-tuple-element.26.att_hbm, f32[4,128,256]{2,1,0:T(8,128)S(1)} %get-tuple-element.27.node_hbm, bf16[8,128,256]{2,1,0:T(8,128)(2,1)S(1)} %get-tuple-element.28.leaving_ref, ...), custom_call_target="tpu_custom_call" | custom-call | tf_op jit(solution)/shard_map/tail/pallas_call | solution.py:738
  111.8 0.7 copy.22
  112.5 0.8 copy.23
  113.3 0.6 copy.24
  113.8 0.7 copy.25
Async XLA Ops:
  0.6 57.8 %copy-start = (bf16[512,256]{1,0:T(8,128)(2,1)S(1)}, bf16[512,256]{1,0:T(8,128)(2,1)}, u32[]{:S(2)}) copy-start(bf16[512,256]{1,0:T(8,128)(2,1)} %nodes_ref.5) | copy-start | bytes 786436
  0.6 57.8 %copy-start.2 = (bf16[256,256]{1,0:T(8,128)(2,1)S(1)}, bf16[256,256]{1,0:T(8,128)(2,1)}, u32[]{:S(2)}) copy-start(bf16[256,256]{1,0:T(8,128)(2,1)} %wo_ref.5) | copy-start | bytes 393220
  0.7 57.8 %copy-start.1 = (bf16[512,256]{1,0:T(8,128)(2,1)S(1)}, bf16[512,256]{1,0:T(8,128)(2,1)}, u32[]{:S(2)}) copy-start(bf16[512,256]{1,0:T(8,128)(2,1)} %dout_ref.5) | copy-start | bytes 786436
  0.7 57.8 %copy-start.12 = (s32[2,4]{1,0:T(2,128)S(1)}, s32[2,4]{1,0:T(2,128)}, u32[]{:S(2)}) copy-start(s32[2,4]{1,0:T(2,128)} %pairs_ref.5) | copy-start | bytes 100
  0.7 57.8 %copy-start.8 = (bf16[256,128]{1,0:T(8,128)(2,1)S(1)}, bf16[256,128]{1,0:T(8,128)(2,1)}, u32[]{:S(2)}) copy-start(bf16[256,128]{1,0:T(8,128)(2,1)} %wr_ref.3) | copy-start | bytes 196612
  0.7 57.8 %copy-start.7 = (bf16[256,128]{1,0:T(8,128)(2,1)S(1)}, bf16[256,128]{1,0:T(8,128)(2,1)}, u32[]{:S(2)}) copy-start(bf16[256,128]{1,0:T(8,128)(2,1)} %wl_ref.3) | copy-start | bytes 196612
  0.7 57.8 %copy-start.5 = (bf16[256,256]{1,0:T(8,128)(2,1)S(1)}, bf16[256,256]{1,0:T(8,128)(2,1)}, u32[]{:S(2)}) copy-start(bf16[256,256]{1,0:T(8,128)(2,1)} %wv_ref.3) | copy-start | bytes 393220
  0.7 57.8 %copy-start.4 = (bf16[256,256]{1,0:T(8,128)(2,1)S(1)}, bf16[256,256]{1,0:T(8,128)(2,1)}, u32[]{:S(2)}) copy-start(bf16[256,256]{1,0:T(8,128)(2,1)} %wk_ref.3) | copy-start | bytes 393220
  0.7 57.8 %copy-start.3 = (bf16[256,256]{1,0:T(8,128)(2,1)S(1)}, bf16[256,256]{1,0:T(8,128)(2,1)}, u32[]{:S(2)}) copy-start(bf16[256,256]{1,0:T(8,128)(2,1)} %wq_ref.3) | copy-start | bytes 393220
  0.7 57.8 %copy-start.13 = (s32[4,128]{1,0:T(4,128)S(1)}, s32[4,128]{1,0:T(4,128)}, u32[]{:S(2)}) copy-start(s32[4,128]{1,0:T(4,128)} %param.17) | copy-start | bytes 6148
  58.5 1.0 copy-start.6
  59.6 0.8 copy-start.9
  60.4 0.8 copy-start.10
  61.2 23.3 %copy-start.11 = (f32[8,8,128]{2,1,0:T(8,128)S(1)}, f32[8,8,128]{2,1,0:T(8,128)}, u32[]{:S(2)}) copy-start(f32[8,8,128]{2,1,0:T(8,128)} %get-tuple-element.29.asked_ref) | copy-start | bytes 98308
